TPU v7x, 32 devices: a whole 2x2x4 slice. The times are simulated.
32 devices in a mesh: enc: 4 (over z), bin: 4 (over x, core), off: 2 (over y).
Axes of the slice: x: 2, y: 2, z: 4, core: 2. Of those that a mesh axis runs over, the one named last changes fastest.
Arguments:
- encoder_in: bfloat16 [512, 1536], P(('bin', 'off'), 'enc'), may hold values from -6 to 6
- gain_enc: float32 [512], P(('bin', 'off')), may hold values from 0.1 to 1.9
- conv_one: bfloat16 [3, 512, 512], P(None, ('bin', 'off')), may hold values from -0.15625 to 0.15625
- proj_weight: bfloat16 [2, 512, 32], P(None, ('bin', 'off')), may hold values from -0.25 to 0.25
- conv_two: bfloat16 [9, 32, 32], replicated, may hold values from -0.375 to 0.375
- head_weight: float32 [32], replicated, may hold values from -1 to 1
- target: bfloat16 [1536, 1024], P('bin', ('enc', 'off')), may hold values from -8 to 8
- valid_bins: int32 [1536], replicated, may hold values 0 or 1
- offset_limit: int32 [1536], replicated, may hold values from 512 to 1024
- dilations: int32 [2], replicated, may hold values from 1 to 8, as said below
Outputs:
- prediction: float32 [1536, 1024], P('bin', ('enc', 'off'))
- loss_mean: float32 [1], replicated
- grad_conv_two: float32 [9, 32, 32], replicated
- grad_proj: float32 [2, 512, 32], P(None, ('bin', 'off'))
- grad_conv_one: float32 [3, 512, 512], P(None, ('bin', 'off'), 'enc')
Inputs may be any that keep to these rules, and one draw needn't show every extreme that they name: dilations[0] is the dilation of the 1-D layer and dilations[1] that of the 2-D layer; one of the two equals 8, the other is smaller.
All inputs are finite; a program needn't handle non-finite values.
Results may differ from a plain program's by a relative error of at most 0.0013.
The roundings to bfloat16 on the way count: a program that leaves them out, or rounds other values in their place, can miss the bound.
Values may be sent and summed in bfloat16 or wider, within the bound.
A program may use at most 192 MiB of HBM per device.

v0:
```python
import jax
import jax.numpy as jnp
from jax import lax
from jax.sharding import PartitionSpec as P

LARGEST_DILATION = 8


def with_halo(cells, sides, width):
    for axis, dim in sides:
        count = lax.axis_size(axis)
        ends = count - 1
        head = lax.slice_in_dim(cells, 0, width, axis=dim)
        tail = lax.slice_in_dim(cells, cells.shape[dim] - width, cells.shape[dim], axis=dim)
        cells = jnp.concatenate(
            [
                lax.ppermute(tail, axis, [(i, (i + 1) % count) for i in range(ends)]),
                cells,
                lax.ppermute(head, axis, [((i + 1) % count, i) for i in range(ends)]),
            ],
            axis=dim,
        )
    return cells


def hankel(window, tile_rows, tile_cols):
    chans = window.shape[0]
    width = tile_rows + tile_cols
    base = window[:, : width - 1]
    tiled = jnp.broadcast_to(base[:, None, :], (chans, tile_rows, width - 1)).reshape(
        chans, tile_rows * (width - 1)
    )
    tiled = jnp.pad(tiled, ((0, 0), (0, tile_rows)))
    return tiled.reshape(chans, tile_rows, width)[:, :, :tile_cols]


def diagonal_sums(tile):
    chans, tile_rows, tile_cols = tile.shape
    width = tile_rows + tile_cols
    padded_input = jnp.pad(tile, ((0, 0), (0, 0), (0, tile_rows)))
    flat = padded_input.reshape(chans, tile_rows * width)[:, : tile_rows * (width - 1)]
    return jnp.sum(flat.reshape(chans, tile_rows, width - 1), axis=1)


def count_cells(valid_bins, offset_limit):
    sequence_length = valid_bins.shape[0]
    running = jnp.concatenate([jnp.zeros((1,), jnp.int32), jnp.cumsum(valid_bins)])
    places = jnp.arange(sequence_length, dtype=jnp.int32)
    farthest = jnp.minimum(places + offset_limit, sequence_length)
    inside = jnp.take(running, farthest) - jnp.take(running, places)
    return jnp.sum(valid_bins * inside).astype(jnp.float32)


def shards(
    encoder_in,
    gain_enc,
    conv_one,
    proj_weight,
    conv_two,
    head_weight,
    target,
    valid_bins,
    offset_limit,
    dilations,
):
    chans, encoder_bins = encoder_in.shape
    width_in = conv_one.shape[2]
    second_channels = conv_two.shape[1]
    tile_rows, tile_cols = target.shape
    area = tile_rows * tile_cols
    first_dilation = dilations[0]
    second_dilation = dilations[1]
    activ = jax.nn.gelu(gain_enc[:, None] * encoder_in.astype(jnp.float32)).astype(jnp.bfloat16)
    framed = with_halo(activ, (("enc", 1),), LARGEST_DILATION)
    channel_count = lax.all_gather(framed, ("bin", "off"), axis=0, tiled=True)
    stacked_enc = jnp.concatenate(
        [
            lax.dynamic_slice_in_dim(
                channel_count,
                LARGEST_DILATION + (kernel_tap_index - 1) * first_dilation,
                encoder_bins,
                1,
            )
            for kernel_tap_index in range(3)
        ],
        axis=0,
    )
    weight_one = jnp.transpose(conv_one, (1, 0, 2)).reshape(chans, 3 * width_in)
    conv_out = jnp.dot(weight_one, stacked_enc, preferred_element_type=jnp.float32)
    hidden = (encoder_in.astype(jnp.float32) + conv_out).astype(jnp.bfloat16)
    proj_rows = jnp.transpose(proj_weight, (0, 2, 1)).reshape(2 * second_channels, chans)
    partial_embed = jnp.dot(proj_rows, hidden, preferred_element_type=jnp.float32)
    summed = lax.psum(partial_embed, ("bin", "off")).astype(jnp.bfloat16)
    embed = lax.all_gather(summed, "enc", axis=1, tiled=True)
    sequence_length = embed.shape[1]
    window_extent = tile_cols * lax.axis_size("enc") * lax.axis_size("off")
    row_start = lax.axis_index("bin") * tile_rows
    offs_start = (lax.axis_index("enc") * lax.axis_size("off") + lax.axis_index("off")) * tile_cols
    near_rows = lax.dynamic_slice_in_dim(embed[:second_channels], row_start, tile_rows, 1)
    far_ext = jnp.concatenate(
        [embed[second_channels:], jnp.zeros((second_channels, window_extent), jnp.bfloat16)], axis=1
    )
    far_window = lax.dynamic_slice_in_dim(far_ext, row_start + offs_start, tile_rows + tile_cols, 1)
    pair_sum = near_rows[:, :, None].astype(jnp.float32) + hankel(
        far_window, tile_rows, tile_cols
    ).astype(jnp.float32)
    band_act = jnp.maximum(pair_sum, 0.0).astype(jnp.bfloat16)
    shifts = [
        (bin_displacement, offset_displacement)
        for bin_displacement in (-1, 0, 1)
        for offset_displacement in (-1, 0, 1)
    ]
    framed_band = with_halo(band_act, (("bin", 1), (("enc", "off"), 2)), LARGEST_DILATION)
    stacked_band = jnp.concatenate(
        [
            lax.dynamic_slice(
                framed_band,
                (
                    0,
                    LARGEST_DILATION + bin_displacement * second_dilation,
                    LARGEST_DILATION + offset_displacement * second_dilation,
                ),
                (second_channels, tile_rows, tile_cols),
            ).reshape(second_channels, area)
            for bin_displacement, offset_displacement in shifts
        ],
        axis=0,
    )
    weight_fwd = jnp.transpose(conv_two, (2, 0, 1)).reshape(second_channels, 9 * second_channels)
    band_conv = jnp.dot(weight_fwd, stacked_band, preferred_element_type=jnp.float32).reshape(
        second_channels, tile_rows, tile_cols
    )
    resid = pair_sum + band_conv
    prediction = jnp.sum(head_weight[:, None, None] * jnp.maximum(resid, 0.0), axis=0)
    mask_float = valid_bins.astype(jnp.float32)
    mask_ext = jnp.concatenate([mask_float, jnp.zeros((window_extent,), jnp.float32)])
    mask_near = lax.dynamic_slice_in_dim(mask_float, row_start, tile_rows)
    mask_far = hankel(
        lax.dynamic_slice_in_dim(mask_ext, row_start + offs_start, tile_rows + tile_cols)[None, :],
        tile_rows,
        tile_cols,
    )[0]
    limit_near = lax.dynamic_slice_in_dim(offset_limit, row_start, tile_rows)
    offs_ids = offs_start + jnp.arange(tile_cols, dtype=jnp.int32)
    weight = (
        mask_near[:, None]
        * mask_far
        * (offs_ids[None, :] < limit_near[:, None]).astype(jnp.float32)
    )
    denom = 1.0 + count_cells(valid_bins, offset_limit)
    differ = prediction - target.astype(jnp.float32)
    error_sum = jnp.sum(weight * differ * differ)
    dpred = 2.0 * weight * differ / denom
    dres = (head_weight[:, None, None] * dpred[None] * (resid > 0.0).astype(jnp.float32)).astype(
        jnp.bfloat16
    )
    grad_band = lax.dot_general(
        stacked_band,
        dres.reshape(second_channels, area),
        (((1,), (1,)), ((), ())),
        preferred_element_type=jnp.float32,
    ).reshape(9, second_channels, second_channels)
    framed_grad = with_halo(dres, (("bin", 1), (("enc", "off"), 2)), LARGEST_DILATION)
    stacked_grad = jnp.concatenate(
        [
            lax.dynamic_slice(
                framed_grad,
                (
                    0,
                    LARGEST_DILATION - bin_displacement * second_dilation,
                    LARGEST_DILATION - offset_displacement * second_dilation,
                ),
                (second_channels, tile_rows, tile_cols),
            ).reshape(second_channels, area)
            for bin_displacement, offset_displacement in shifts
        ],
        axis=0,
    )
    weight_back = jnp.transpose(conv_two, (1, 0, 2)).reshape(second_channels, 9 * second_channels)
    dact = jnp.dot(weight_back, stacked_grad, preferred_element_type=jnp.float32).reshape(
        second_channels, tile_rows, tile_cols
    )
    dpair = dres.astype(jnp.float32) + dact * (pair_sum > 0.0).astype(jnp.float32)
    near_grad = jnp.sum(dpair, axis=2)
    far_grad = diagonal_sums(dpair)
    enc_start = lax.axis_index("enc") * encoder_bins
    buffer = jnp.zeros((2, second_channels, sequence_length + window_extent), jnp.float32)
    buffer = lax.dynamic_update_slice(buffer, near_grad[None], (0, 0, row_start))
    buffer = lax.dynamic_update_slice(buffer, far_grad[None], (1, 0, row_start + offs_start))
    buffer = buffer[:, :, :sequence_length]
    grad_whole, grad_conv_two, total_error = lax.psum(
        (buffer, grad_band, error_sum), ("enc", "bin", "off")
    )
    grad_embed = lax.dynamic_slice_in_dim(grad_whole, enc_start, encoder_bins, 2).astype(
        jnp.bfloat16
    )
    grad_rows = grad_embed.reshape(2 * second_channels, encoder_bins)
    dhidden = jnp.dot(proj_rows.T, grad_rows, preferred_element_type=jnp.float32).astype(
        jnp.bfloat16
    )
    proj_local = jnp.dot(hidden, grad_rows.T, preferred_element_type=jnp.float32)
    proj_local = jnp.transpose(proj_local.reshape(chans, 2, second_channels), (1, 0, 2))
    conv_local = lax.dot_general(
        dhidden, stacked_enc, (((1,), (1,)), ((), ())), preferred_element_type=jnp.float32
    )
    conv_local = jnp.transpose(conv_local.reshape(chans, 3, width_in), (1, 0, 2))
    grad_proj = lax.psum(proj_local, "enc")
    grad_conv_one = lax.psum_scatter(conv_local, "enc", scatter_dimension=2, tiled=True)
    loss_mean = (total_error / denom).reshape(1)
    return (prediction, loss_mean, grad_conv_two, grad_proj, grad_conv_one)


def solution(mesh):
    in_specs = (
        P(("bin", "off"), "enc"),
        P(("bin", "off")),
        P(None, ("bin", "off"), None),
        P(None, ("bin", "off"), None),
        P(),
        P(),
        P("bin", ("enc", "off")),
        P(),
        P(),
        P(),
    )
    out_specs = (
        P("bin", ("enc", "off")),
        P(),
        P(),
        P(None, ("bin", "off"), None),
        P(None, ("bin", "off"), "enc"),
    )
    return jax.shard_map(shards, mesh=mesh, in_specs=in_specs, out_specs=out_specs, check_vma=False)
```

profile of v0, /device:TPU:0, one launch (start us, length us, event | category | flops | bytes accessed | tf_op | source)
XLA Modules:
  0.0 674.4 jit_solution(9460276068114126527)
XLA Ops:
  9.5 5.6 collective-permute-start
  21.4 8.4 %gather_fusion.1 = s32[1536]{0:T(1024)S(1)} fusion(s32[1537]{0:T(1024)S(1)} %pad_add_fusion, s32[2048]{0:T(1024)S(1)} %get-tuple-element.73), kind=kCustom, calls=%fused_computation.1.clone | custom fusion | bytes 18432 | tf_op jit(solution)/shard_map/jit(_take)/gather | solution.py:50
  29.8 8.4 %gather_fusion = s32[1536]{0:T(1024)S(1)} fusion(s32[1537]{0:T(1024)S(1)} %pad_add_fusion, s32[2048]{0:T(1024)S(1)} %get-tuple-element.74), kind=kCustom, calls=%fused_computation.clone | custom fusion | bytes 18432 | tf_op jit(solution)/shard_map/jit(_take)/gather | solution.py:50
  38.3 17.9 %all_gather.6 = bf16[512,400]{1,0:T(8,128)(2,1)S(1)} all-gather(bf16[64,400]{1,0:T(8,128)(2,1)S(1)} %pad_maximum_fusion.7), channel_id=1, replica_groups=mesh['enc'=4,'bin'=4,'off'=2] {'bin','off'}, dimensions={0}, use_global_device_ids=true | all-gather | bytes 460800 | tf_op jit(solution)/shard_map/all_gather | solution.py:75
  58.3 25.2 %psum.35 = bf16[64,384]{1,0:T(8,128)(2,1)S(1)} all-reduce(f32[64,384]{1,0:T(8,128)S(1)} %convolution_bitcast_fusion.3), channel_id=1, replica_groups=mesh['enc'=4,'bin'=4,'off'=2] {'bin','off'}, use_global_device_ids=true, to_apply=%region_0.0 | all-reduce | flops 24576 | bytes 147456 | tf_op jit(solution)/shard_map/psum | solution.py:93
  83.5 14.0 %all_gather.7 = bf16[64,1536]{1,0:T(8,128)(2,1)S(1)} all-gather(bf16[64,384]{1,0:T(8,128)(2,1)S(1)} %psum.35), channel_id=1, replica_groups=mesh['enc'=4,'bin'=4,'off'=2] {'enc'}, dimensions={1}, use_global_device_ids=true | all-gather | bytes 245760 | tf_op jit(solution)/shard_map/all_gather | solution.py:94
  97.6 5.5 broadcast_in_dim.22
  103.1 21.3 %reshape.186 = bf16[32,196224]{1,0:T(8,128)(2,1)} reshape(bf16[32,384,511]{2,1,0:T(8,128)(2,1)} %broadcast_in_dim.22) | data formatting | bytes 25116672 | tf_op jit(solution)/shard_map/reshape | solution.py:30
  124.4 6.1 pad.14
  130.5 11.2 %copy.89 = bf16[4,8,384,512]{3,2,1,0:T(8,128)(2,1)S(1)} copy(bf16[4,8,384,512]{3,1,2,0:T(8,128)(2,1)S(1)} %bitcast.166) | data formatting | bytes 25165824
  166.8 5.4 collective-permute-start.4
  179.4 10.0 %pad_reduce_fusion = f32[196608]{0:T(1024)} fusion(f32[1,196224]{1,0:T(1,128)} %broadcast_in_dim.48), kind=kLoop, calls=%fused_computation.43 | loop fusion | bytes 1571328 | tf_op jit(solution)/shard_map/jit(_pad)/pad | solution.py:33
  202.4 8.9 %pad_maximum_fusion = bf16[32,400,144]{2,1,0:T(8,128)(2,1)} fusion(bf16[32,400,8]{2,1,0:T(8,128)(2,1)} %copy.71, bf16[32,8,128]{2,1,0:T(8,128)(2,1)S(1)} %collective-permute-done.3, bf16[32,384,128]{2,1,0:T(8,128)(2,1)S(1)} %maximum_convert_fusion, bf16[32,8,128]{2,1,0:T(8,128)(2,1)S(1)} %collective-permute-done.2, bf16[32,400,8]{2,1,0:T(8,128)(2,1)} %copy.70), kind=kLoop, calls=%fused_computation.2 | loop fusion | flops 18432000 | bytes 7372800 | tf_op jit(solution)/shard_map/concatenate | solution.py:15
  211.3 37.2 %constant_dynamic-slice_fusion.8 = (bf16[32,384,128]{2,1,0:T(8,128)(2,1)}, bf16[32,384,128]{2,1,0:T(8,128)(2,1)}, bf16[32,384,128]{2,1,0:T(8,128)(2,1)}, bf16[32...) fusion(bf16[32,400,144]{2,1,0:T(8,128)(2,1)} %pad_maximum_fusio, ...), kind=kLoop, calls=%fused_computation.87 | loop fusion | bytes 50331664 | tf_op jit(solution)/shard_map/dynamic_slice | solution.py:116
  248.5 5.5 bitcast_dynamic-update-slice_fusion.17
  282.3 11.8 %convolution_bitcast_fusion.1 = f32[4,8,384,128]{3,1,2,0:T(8,128)S(1)} fusion(bf16[288,49152]{1,0:T(8,128)(2,1)} %bitcast_dynamic-update-slice_fusion.9, bf16[32,288]{0,1:T(8,128)(2,1)S(1)} %bitcast.185), kind=kOutput, calls=%fused_computation.33 | convolution fusion | flops 905969664 | bytes 34621440 | tf_op jit(solution)/shard_map/dot_general | solution.py:130
  337.9 14.4 %fusion.35 = f32[9,32,32]{2,1,0:T(8,128)} fusion(bf16[9,32,49152]{2,1,0:T(8,128)(2,1)} %bitcast.24, bf16[32,49152,1]{1,0,2:T(8,128)(2,1)} %reshape.239), kind=kOutput, calls=%fused_computation.108 | convolution fusion | flops 905969664 | bytes 31494144 | tf_op jit(solution)/shard_map/dot_general | solution.py:157
  359.6 8.9 %pad_maximum_fusion.1 = bf16[32,400,144]{2,1,0:T(8,128)(2,1)} fusion(bf16[32,400,8]{2,1,0:T(8,128)(2,1)} %copy.79, bf16[32,8,128]{2,1,0:T(8,128)(2,1)S(1)} %collective-permute-done.7, bf16[32,384,128]{2,1,0:T(8,128)(2,1)S(1)} %select_convert_fusion, bf16[32,8,128]{2,1,0:T(8,128)(2,1)S(1)} %collective-permute-done.6, bf16[32,400,8]{2,1,0:T(8,128)(2,1)} %copy.78), kind=kLoop, calls=%fused_computation.3 | loop fusion | flops 18432000 | bytes 7372800 | tf_op jit(solution)/shard_map/concatenate | solution.py:15
  368.5 37.0 %constant_dynamic-slice_fusion = (bf16[32,384,128]{2,1,0:T(8,128)(2,1)}, bf16[32,384,128]{2,1,0:T(8,128)(2,1)}, bf16[32,384,128]{2,1,0:T(8,128)(2,1)}, bf16[32,3...) fusion(bf16[32,400,144]{2,1,0:T(8,128)(2,1)} %pad_maximum_fusio, ...), kind=kLoop, calls=%fused_computation.79 | loop fusion | bytes 50331664 | tf_op jit(solution)/shard_map/dynamic_slice | solution.py:166
  405.5 5.5 bitcast_dynamic-update-slice_fusion.8
  439.5 11.8 %convolution_bitcast_fusion = f32[4,8,384,128]{3,1,2,0:T(8,128)S(1)} fusion(bf16[288,49152]{1,0:T(8,128)(2,1)} %bitcast_dynamic-update-slice_fusion, bf16[32,288]{0,1:T(8,128)(2,1)S(1)} %bitcast.187), kind=kOutput, calls=%fused_computation.32 | convolution fusion | flops 905969664 | bytes 34621440 | tf_op jit(solution)/shard_map/dot_general | solution.py:180
  452.4 6.8 %fusion.26 = (f32[32,384]{1,0:T(8,128)S(1)}, f32[32,384,128]{2,1,0:T(8,128)}) fusion(f32[4,8,384,128]{3,2,1,0:T(8,128)S(1)} %copy.109, bf16[32,384,512]{2,1,0:T(8,128)(2,1)} %bitcast.165, f32[32,384]{1,0:T(8,128)S(1)} %dynamic-slice_convert_fusion.1, bf16[32,384,128]{2,1,0:T(8,128)(2,1)S(1)} %select_convert_fusion), kind=kLoop, calls=%fused_computation.100 | loop fusion | flops 10997760 | bytes 18972672 | tf_op jit(solution)/shard_map/reduce_sum | solution.py:184
  459.3 14.4 %pad.16 = f32[32,384,512]{2,1,0:T(8,128)} pad(f32[32,384,128]{2,1,0:T(8,128)} %get-tuple-element.35, f32[]{:T(128)} %constant.95.clone.1), padding=0_0x0_0x0_384 | pad | bytes 31457284 | tf_op jit(solution)/shard_map/jit(_pad)/pad | solution.py:40
  473.7 21.9 %copy.110 = f32[4,8,384,512]{3,1,2,0:T(8,128)S(1)} copy(f32[4,8,384,512]{3,2,1,0:T(8,128)} %bitcast.158) | data formatting | bytes 50331648
  495.6 8.6 %slice.110 = f32[32,196224]{1,0:T(8,128)} slice(f32[32,196608]{1,0:T(8,128)S(1)} %bitcast.159), slice={[0:32], [0:196224]} | slice | bytes 50233344 | tf_op jit(solution)/shard_map/slice | solution.py:41
  504.2 43.9 %reshape.215 = f32[32,384,511]{2,1,0:T(8,128)} reshape(f32[32,196224]{1,0:T(8,128)} %slice.110) | data formatting | bytes 50233344 | tf_op jit(solution)/shard_map/reshape | solution.py:42
  548.1 10.1 %reduce_sum.49 = f32[32,511]{1,0:T(8,128)S(1)} reduce(f32[32,384,511]{2,1,0:T(8,128)} %reshape.215, f32[]{:T(128)} %constant.95.clone.1), dimensions={1}, to_apply=%region_9.11 | reduce | flops 6262816 | bytes 25182084 | tf_op jit(solution)/shard_map/reduce_sum | solution.py:42
  559.0 47.5 %all-reduce.7 = (f32[]{:T(128)}, f32[9,32,32]{2,1,0:T(8,128)}, bf16[2,32,1536]{2,1,0:T(8,128)(2,1)S(1)}) all-reduce(f32[]{:T(128)} %get-tuple-element.64, f32[9,32,32]{2,1,0:T(8,128)S(1)} %copy-done.28, f32[2,32,1536]{2,1,0:T(8,128)S(1)} %slice.111), channel_id=1, replica_groups=mesh['enc'=4,'bin'=4,'off'=2] {'enc','bin','off'}, use_global_device_ids=true, to_apply=%region_3.4 | all-reduce | flops 107521 | bytes 663560 | tf_op jit(solution)/shard_map/psum | solution.py:191
  607.4 13.8 %copy.83 = f32[3,64,512]{0,1,2:T(8,128)} copy(f32[3,64,512]{2,0,1:T(4,128)S(1)} %bitcast.184) | data formatting | bytes 786432
  621.2 13.3 %reshape.243 = f32[512,192]{1,0:T(8,128)} reshape(f32[512,64,3]{2,1,0:T(8,128)} %bitcast.160) | data formatting | bytes 786432
  635.4 18.6 %psum.39 = f32[2,64,32]{1,2,0:T(8,128)} all-reduce(f32[2,64,32]{1,2,0:T(8,128)S(1)} %convolution_bitcast_fusion.5), channel_id=1, replica_groups=mesh['enc'=4,'bin'=4,'off'=2] {'enc'}, use_global_device_ids=true, to_apply=%region_11.13 | all-reduce | flops 4096 | bytes 32768 | tf_op jit(solution)/shard_map/psum | solution.py:207
  655.4 6.4 reshape.244
  (166 shorter events, 165.2 us)
Async XLA Ops:
  7.2 50.3 %copy-start = (bf16[2,64,32]{1,2,0:T(8,128)(2,1)S(1)}, bf16[2,64,32]{1,2,0:T(8,128)(2,1)}, u32[]{:S(2)}) copy-start(bf16[2,64,32]{1,2,0:T(8,128)(2,1)} %param.15) | copy-start | bytes 24580
  7.2 648.2 %reduce-scatter.4.cloned.1.call-start = ((), (), s32[]{:S(2)}) async-start(), calls=%async_computation.1 | async-start | bytes 655360
  8.2 30.0 %collective-permute-start.1 = (bf16[64,8]{1,0:T(8,128)(2,1)S(1)}, bf16[64,8]{1,0:T(8,128)(2,1)S(1)}, u32[]{:S(2)}, u32[]{:S(2)}) collective-permute-start(bf16[64,8]{1,0:T(8,128)(2,1)S(1)} %get-tuple-element.68), channel_id=1, source_target_pairs={{8,0},{16,8},{24,16},{9,1},{17,9},{25,17},{10,2},{18,10},{26,18},{... | collective-permute-start | bytes 3080 | tf_op jit(solution)/shard_map/ppermute | solution.py:19
  9.5 28.7 %collective-permute-start = (bf16[64,8]{1,0:T(8,128)(2,1)S(1)}, bf16[64,8]{1,0:T(8,128)(2,1)S(1)}, u32[]{:S(2)}, u32[]{:S(2)}) collective-permute-start(bf16[64,8]{1,0:T(8,128)(2,1)S(1)} %get-tuple-element.67), channel_id=1, source_target_pairs={{0,8},{8,16},{16,24},{1,9},{9,17},{17,25},{2,10},{10,18},{18,26},{... | collective-permute-start | bytes 3080 | tf_op jit(solution)/shard_map/ppermute | solution.py:17
  29.8 27.0 %copy-start.29 = (bf16[64,384]{1,0:T(8,128)(2,1)S(1)}, bf16[64,384]{1,0:T(8,128)(2,1)}, u32[]{:S(2)}) copy-start(bf16[64,384]{1,0:T(8,128)(2,1)} %param.12) | copy-start | bytes 147460
  141.8 10.8 %copy-start.30 = (s32[1536]{0:T(1024)S(1)}, s32[1536]{0:T(1024)}, u32[]{:S(2)}) copy-start(s32[1536]{0:T(1024)} %param.20) | copy-start | bytes 18436
  141.8 10.8 %copy-start.31 = (s32[1536]{0:T(1024)S(1)}, s32[1536]{0:T(1024)}, u32[]{:S(2)}) copy-start(s32[1536]{0:T(1024)} %param.19) | copy-start | bytes 18436
  148.2 5.1 collective-permute-start.3
  149.5 3.9 collective-permute-start.2
  161.5 33.5 %collective-permute-start.5 = (bf16[32,400,8]{1,2,0:T(8,128)(2,1)}, bf16[32,400,8]{1,2,0:T(8,128)(2,1)}, u32[]{:S(2)}, u32[]{:S(2)}) collective-permute-start(bf16[32,400,8]{1,2,0:T(8,128)(2,1)} %copy.69), channel_id=1, source_target_pairs={{1,0},{8,1},{9,8},{16,9},{17,16},{24,17},{25,24},{3,2},{10,3},{11,... | collective-permute-start | bytes 614408 | tf_op jit(solution)/shard_map/ppermute | solution.py:19
  166.8 31.9 %collective-permute-start.4 = (bf16[32,400,8]{1,2,0:T(8,128)(2,1)}, bf16[32,400,8]{1,2,0:T(8,128)(2,1)}, u32[]{:S(2)}, u32[]{:S(2)}) collective-permute-start(bf16[32,400,8]{1,2,0:T(8,128)(2,1)} %copy.68), channel_id=1, source_target_pairs={{0,1},{1,8},{8,9},{9,16},{16,17},{17,24},{24,25},{2,3},{3,10},{10,... | collective-permute-start | bytes 614408 | tf_op jit(solution)/shard_map/ppermute | solution.py:17
  248.5 9.0 %copy-start.13 = (bf16[32,384,128]{2,1,0:T(8,128)(2,1)S(1)}, bf16[32,384,128]{2,1,0:T(8,128)(2,1)}, u32[]{:S(2)}) copy-start(bf16[32,384,128]{2,1,0:T(8,128)(2,1)} %get-tuple-element.49) | copy-start | bytes 9437188
  254.0 7.0 %copy-start.11 = (bf16[32,384,128]{2,1,0:T(8,128)(2,1)S(1)}, bf16[32,384,128]{2,1,0:T(8,128)(2,1)}, u32[]{:S(2)}) copy-start(bf16[32,384,128]{2,1,0:T(8,128)(2,1)} %get-tuple-element.48) | copy-start | bytes 9437188
  261.0 7.0 %copy-start.9 = (bf16[32,384,128]{2,1,0:T(8,128)(2,1)S(1)}, bf16[32,384,128]{2,1,0:T(8,128)(2,1)}, u32[]{:S(2)}) copy-start(bf16[32,384,128]{2,1,0:T(8,128)(2,1)} %get-tuple-element.47) | copy-start | bytes 9437188
  264.5 6.9 %copy-start.7 = (bf16[32,384,128]{2,1,0:T(8,128)(2,1)S(1)}, bf16[32,384,128]{2,1,0:T(8,128)(2,1)}, u32[]{:S(2)}) copy-start(bf16[32,384,128]{2,1,0:T(8,128)(2,1)} %get-tuple-element.46) | copy-start | bytes 9437188
  268.0 7.2 %copy-start.5 = (bf16[32,384,128]{2,1,0:T(8,128)(2,1)S(1)}, bf16[32,384,128]{2,1,0:T(8,128)(2,1)}, u32[]{:S(2)}) copy-start(bf16[32,384,128]{2,1,0:T(8,128)(2,1)} %get-tuple-element.45) | copy-start | bytes 9437188
  271.5 7.3 %copy-start.3 = (bf16[32,384,128]{2,1,0:T(8,128)(2,1)S(1)}, bf16[32,384,128]{2,1,0:T(8,128)(2,1)}, u32[]{:S(2)}) copy-start(bf16[32,384,128]{2,1,0:T(8,128)(2,1)} %get-tuple-element.44) | copy-start | bytes 9437188
  275.2 7.0 %copy-start.25 = (bf16[9,32,32]{2,1,0:T(8,128)(2,1)S(1)}, bf16[9,32,32]{2,1,0:T(8,128)(2,1)}, u32[]{:S(2)}) copy-start(bf16[9,32,32]{2,1,0:T(8,128)(2,1)} %param.16) | copy-start | bytes 55300
  309.5 9.8 %collective-permute-start.7 = (bf16[32,8,128]{2,1,0:T(8,128)(2,1)}, bf16[32,8,128]{2,1,0:T(8,128)(2,1)S(1)}, u32[]{:S(2)}, u32[]{:S(2)}) collective-permute-start(bf16[32,8,128]{2,1,0:T(8,128)(2,1)} %get-tuple-element.57), channel_id=1, source_target_pairs={{2,0},{4,2},{6,4},{3,1},{5,3},{7,5},{10,8},{12,10},{14,12},{11,9},... | collective-permute-start | bytes 196616 | tf_op jit(solution)/shard_map/ppermute | solution.py:19
  310.8 8.5 %collective-permute-start.6 = (bf16[32,8,128]{2,1,0:T(8,128)(2,1)}, bf16[32,8,128]{2,1,0:T(8,128)(2,1)S(1)}, u32[]{:S(2)}, u32[]{:S(2)}) collective-permute-start(bf16[32,8,128]{2,1,0:T(8,128)(2,1)} %get-tuple-element.56), channel_id=1, source_target_pairs={{0,2},{2,4},{4,6},{1,3},{3,5},{5,7},{8,10},{10,12},{12,14},{9,11},... | collective-permute-start | bytes 196616 | tf_op jit(solution)/shard_map/ppermute | solution.py:17
  327.4 24.9 %collective-permute-start.9 = (bf16[32,400,8]{1,2,0:T(8,128)(2,1)}, bf16[32,400,8]{1,2,0:T(8,128)(2,1)}, u32[]{:S(2)}, u32[]{:S(2)}) collective-permute-start(bf16[32,400,8]{1,2,0:T(8,128)(2,1)} %copy.77), channel_id=1, source_target_pairs={{1,0},{8,1},{9,8},{16,9},{17,16},{24,17},{25,24},{3,2},{10,3},{11,... | collective-permute-start | bytes 614408 | tf_op jit(solution)/shard_map/ppermute | solution.py:19
  332.7 23.3 %collective-permute-start.8 = (bf16[32,400,8]{1,2,0:T(8,128)(2,1)}, bf16[32,400,8]{1,2,0:T(8,128)(2,1)}, u32[]{:S(2)}, u32[]{:S(2)}) collective-permute-start(bf16[32,400,8]{1,2,0:T(8,128)(2,1)} %copy.76), channel_id=1, source_target_pairs={{0,1},{1,8},{8,9},{9,16},{16,17},{17,24},{24,25},{2,3},{3,10},{10,... | collective-permute-start | bytes 614408 | tf_op jit(solution)/shard_map/ppermute | solution.py:17
  405.5 9.0 %copy-start.14 = (bf16[32,384,128]{2,1,0:T(8,128)(2,1)S(1)}, bf16[32,384,128]{2,1,0:T(8,128)(2,1)}, u32[]{:S(2)}) copy-start(bf16[32,384,128]{2,1,0:T(8,128)(2,1)} %get-tuple-element.41) | copy-start | bytes 9437188
  411.0 7.0 %copy-start.12 = (bf16[32,384,128]{2,1,0:T(8,128)(2,1)S(1)}, bf16[32,384,128]{2,1,0:T(8,128)(2,1)}, u32[]{:S(2)}) copy-start(bf16[32,384,128]{2,1,0:T(8,128)(2,1)} %get-tuple-element.40) | copy-start | bytes 9437188
  418.1 7.0 %copy-start.10 = (bf16[32,384,128]{2,1,0:T(8,128)(2,1)S(1)}, bf16[32,384,128]{2,1,0:T(8,128)(2,1)}, u32[]{:S(2)}) copy-start(bf16[32,384,128]{2,1,0:T(8,128)(2,1)} %get-tuple-element.39) | copy-start | bytes 9437188
  425.0 7.4 %copy-start.6 = (bf16[32,384,128]{2,1,0:T(8,128)(2,1)S(1)}, bf16[32,384,128]{2,1,0:T(8,128)(2,1)}, u32[]{:S(2)}) copy-start(bf16[32,384,128]{2,1,0:T(8,128)(2,1)} %get-tuple-element.37) | copy-start | bytes 9437188
  428.5 7.4 %copy-start.4 = (bf16[32,384,128]{2,1,0:T(8,128)(2,1)S(1)}, bf16[32,384,128]{2,1,0:T(8,128)(2,1)}, u32[]{:S(2)}) copy-start(bf16[32,384,128]{2,1,0:T(8,128)(2,1)} %get-tuple-element.36) | copy-start | bytes 9437188
  548.1 10.9 %copy-start.28 = (f32[9,32,32]{2,1,0:T(8,128)S(1)}, f32[9,32,32]{2,1,0:T(8,128)}, u32[]{:S(2)}) copy-start(f32[9,32,32]{2,1,0:T(8,128)} %fusion.35) | copy-start | bytes 110596
  548.1 58.4 %copy-start.20 = (bf16[512,384]{1,0:T(8,128)(2,1)S(1)}, bf16[512,384]{1,0:T(8,128)(2,1)}, u32[]{:S(2)}) copy-start(bf16[512,384]{1,0:T(8,128)(2,1)} %copy-done.19) | copy-start | bytes 1179652
  548.1 58.4 %copy-start.22 = (bf16[512,384]{1,0:T(8,128)(2,1)S(1)}, bf16[512,384]{1,0:T(8,128)(2,1)}, u32[]{:S(2)}) copy-start(bf16[512,384]{1,0:T(8,128)(2,1)} %copy-done.21) | copy-start | bytes 1179652
  548.1 58.4 %copy-start.24 = (bf16[512,384]{1,0:T(8,128)(2,1)S(1)}, bf16[512,384]{1,0:T(8,128)(2,1)}, u32[]{:S(2)}) copy-start(bf16[512,384]{1,0:T(8,128)(2,1)} %copy-done.23) | copy-start | bytes 1179652
  621.2 14.0 %copy-start.27 = (bf16[64,384]{1,0:T(8,128)(2,1)S(1)}, bf16[64,384]{1,0:T(8,128)(2,1)}, u32[]{:S(2)}) copy-start(bf16[64,384]{1,0:T(8,128)(2,1)} %copy-done.26) | copy-start | bytes 147460
  (12 other events, 38.0 us)
Sparse Core Ops, SparseCore 0:
  634.7 20.6 reduce-scatter.3
where the time goes:
time: 684 us; the launch traced here: 674 us
  local copies, waits for them, and re-layouts  407 us (60%)
  blocking collectives  123 us (18%)
  other arithmetic  50.8 us (7%)
  matrix products  39.1 us (6%)
  starting transfers between devices  28.9 us (4%)
  between operations  23.9 us (3%)
    unnamed x93, local copies, waits for them, and re-layouts  145 us
    psum x1, blocking collectives, shards(): lax.psum((buffer, grad_band, error_sum), ('enc', 'bin', 'off'))  47.5 us
    reshape x1, local copies, waits for them, and re-layouts, diagonal_sums(): return jnp.sum(flat.reshape(chans, tile_rows, width - 1), axis=1)  43.9 us
    dynamic_slice x1, local copies, waits for them, and re-layouts, shards(): lax.dynamic_slice(framed_band, (0, LARGEST_DILATION + bin_displacement *...  37.2 us
    dynamic_slice x1, local copies, waits for them, and re-layouts, shards(): lax.dynamic_slice(framed_grad, (0, LARGEST_DILATION - bin_displacement *...  37 us
    psum x1, blocking collectives, shards(): summed = lax.psum(partial_embed, ('bin', 'off')).astype(jnp.bfloat16)  25.2 us
    ppermute x5, starting transfers between devices, with_halo(): lax.ppermute(tail, axis, [(i, (i + 1) % count) for i in range(ends)])  22.4 us
    reshape x1, local copies, waits for them, and re-layouts, hankel(): jnp.broadcast_to(base[:, None, :], (chans, tile_rows, width - 1))  21.3 us
  transfers between devices with their start and end apart: 11, of which 2 were waited for; matrix products, arithmetic and copies ran while one was open for 11% of the time, Pallas kernels for 0%

commit v1 on v0

v1 whole, which is shorter than its diff:
```python
import functools

import jax
import jax.numpy as jnp
from jax import lax
from jax.experimental import pallas as pl
from jax.experimental.pallas import tpu as pltpu
from jax.sharding import PartitionSpec as P

LARGEST_DILATION = 8


def with_halo(cells, sides, width):
    for axis, dim in sides:
        count = lax.axis_size(axis)
        ends = count - 1
        head = lax.slice_in_dim(cells, 0, width, axis=dim)
        tail = lax.slice_in_dim(cells, cells.shape[dim] - width, cells.shape[dim], axis=dim)
        cells = jnp.concatenate(
            [
                lax.ppermute(tail, axis, [(i, (i + 1) % count) for i in range(ends)]),
                cells,
                lax.ppermute(head, axis, [((i + 1) % count, i) for i in range(ends)]),
            ],
            axis=dim,
        )
    return cells


def count_cells(valid_bins, offset_limit):
    sequence_length = valid_bins.shape[0]
    places = jnp.arange(sequence_length, dtype=jnp.int32)
    gap = places[None, :] - places[:, None]
    scored = (gap >= 0) & (gap < offset_limit[:, None])
    inside = jnp.sum(jnp.where(scored, valid_bins[None, :], 0), axis=1)
    return jnp.sum(valid_bins * inside).astype(jnp.float32)


def round_up(value, step):
    return (value + step - 1) // step * step


def band_body(
    edge,
    rows,
    unroll,
    dil_ref,
    place_ref,
    denom_ref,
    near_ref,
    far_ref,
    fmask_ref,
    lanes_ref,
    limit_ref,
    target_ref,
    head_ref,
    wfwd_ref,
    wback_ref,
    pred_ref,
    err_ref,
    gband_ref,
    gnear_ref,
    gfar_ref,
    far_rolled,
    mask_rolled,
    near_shift,
    stack,
    resid_acc,
    dact_acc,
    own_grad,
):
    chans, width = near_ref.shape
    wide = far_ref.shape[1]
    d = dil_ref[0]
    offs_first = place_ref[0]
    offs_count = place_ref[1]
    denom = denom_ref[0]
    all_rows = rows + 4 * edge
    last = rows + 3 * edge

    def loop(start, stop, body, init):
        def step(index, carry):
            for inner in range(unroll):
                carry = body(start + index * unroll + inner, carry)
            return carry

        return lax.fori_loop(0, (stop - start) // unroll, step, init)

    near_shift[1] = near_ref[...]
    near_shift[0] = pltpu.roll(near_ref[...], d, 1)
    near_shift[2] = pltpu.roll(near_ref[...], width - d, 1)

    def fill(k, carry):
        shift = lax.rem(wide - k, wide)
        far_rolled[k] = pltpu.roll(far_ref[...], shift, 1)[:, :width].astype(jnp.bfloat16)
        mask_rolled[k] = pltpu.roll(fmask_ref[...], shift, 1)[:, :width]
        return carry

    loop(0, all_rows + 2 * edge, fill, 0)

    def clear(r, carry):
        resid_acc[r + edge] = near_ref[...] + far_rolled[r + edge].astype(jnp.float32)
        dact_acc[r] = jnp.zeros((chans, width), jnp.float32)
        return carry

    loop(0, all_rows, clear, 0)
    for r in list(range(edge)) + list(range(last, all_rows)):
        own_grad[r] = jnp.zeros((chans, width), jnp.bfloat16)

    def forward(r, carry):
        offs = offs_first + r - 2 * edge
        inside = jnp.where((offs >= 0) & (offs < offs_count), 1.0, 0.0)
        for a in range(3):
            cells = near_shift[a] + far_rolled[r + edge + (a - 1) * d].astype(jnp.float32)
            cells = jnp.maximum(cells, 0.0) * inside
            stack[r, a * chans : (a + 1) * chans, :] = cells.astype(jnp.bfloat16)
        taps = jnp.dot(wfwd_ref[...], stack[r], preferred_element_type=jnp.float32)
        for b in range(3):
            spot = r + edge - (b - 1) * d
            resid_acc[spot] = resid_acc[spot] + taps[b * chans : (b + 1) * chans]
        return carry

    loop(0, all_rows, forward, 0)

    def middle(r, err):
        resid = resid_acc[r + edge]
        head = head_ref[...]
        pred = jnp.sum(head * jnp.maximum(resid, 0.0), axis=0, keepdims=True)
        pred_ref[pl.ds(r - edge, 1), :] = pred
        offs = offs_first + r - 2 * edge
        inside = jnp.where((offs >= 0) & (offs < offs_count), 1.0, 0.0)
        own_row = jnp.where((r >= 2 * edge) & (r < rows + 2 * edge), 1.0, 0.0)
        weight = (
            lanes_ref[0:1, :]
            * mask_rolled[r + edge][0:1, :]
            * jnp.where(offs < limit_ref[...], inside, 0.0)
        )
        differ = pred - target_ref[pl.ds(r - edge, 1), :]
        own = lanes_ref[1:2, :] * own_row
        err = err + weight * differ * differ * own
        dpred = 2.0 * weight * differ / denom
        dres = jnp.where(resid > 0.0, head * dpred, 0.0).astype(jnp.bfloat16).astype(jnp.float32)
        own_grad[r] = (dres * own).astype(jnp.bfloat16)
        shifted = jnp.concatenate(
            [
                pltpu.roll(dres, width - d, 1).astype(jnp.bfloat16),
                dres.astype(jnp.bfloat16),
                pltpu.roll(dres, d, 1).astype(jnp.bfloat16),
            ],
            axis=0,
        )
        taps = jnp.dot(wback_ref[...], shifted, preferred_element_type=jnp.float32)
        for b in range(3):
            spot = r + (b - 1) * d
            dact_acc[spot] = dact_acc[spot] + taps[b * chans : (b + 1) * chans]
        return err

    err = loop(edge, last, middle, jnp.zeros((1, width), jnp.float32))
    err_ref[...] = err

    def weigh(r, total):
        grads = jnp.concatenate([own_grad[r - (b - 1) * d] for b in range(3)], axis=0)
        return total + lax.dot_general(
            stack[r], grads, (((1,), (1,)), ((), ())), preferred_element_type=jnp.float32
        )

    gband_ref[...] = loop(edge, last, weigh, jnp.zeros((3 * chans, 3 * chans), jnp.float32))

    own_near = jnp.where(lanes_ref[1:2, :] > 0.0, near_ref[...], -jnp.inf)
    gnear_ref[...] = jnp.zeros(gnear_ref.shape, jnp.float32)
    gfar_ref[...] = jnp.zeros(gfar_ref.shape, jnp.float32)
    blank = jnp.zeros((chans, wide - width), jnp.float32)
    near_shift[0] = own_near

    def collect(r, carry):
        pair = near_shift[0] + far_rolled[r + edge].astype(jnp.float32)
        dpair = own_grad[r].astype(jnp.float32) + jnp.where(pair > 0.0, dact_acc[r], 0.0)
        gnear_ref[...] += dpair
        gfar_ref[...] += pltpu.roll(jnp.concatenate([dpair, blank], axis=1), r + edge, 1)
        return carry

    loop(2 * edge, rows + 2 * edge, collect, 0)


def band(near, far, fmask, lanes, limits, target, head, wfwd, wback, dil, place, denom, rows):
    chans, width = near.shape
    wide = far.shape[1]
    edge = LARGEST_DILATION
    all_rows = rows + 4 * edge
    smem = pl.BlockSpec(memory_space=pltpu.SMEM)
    vmem = pl.BlockSpec(memory_space=pltpu.VMEM)
    return pl.pallas_call(
        functools.partial(band_body, edge, rows, 4),
        out_shape=(
            jax.ShapeDtypeStruct((rows + 2 * edge, width), jnp.float32),
            jax.ShapeDtypeStruct((1, width), jnp.float32),
            jax.ShapeDtypeStruct((3 * chans, 3 * chans), jnp.float32),
            jax.ShapeDtypeStruct((chans, width), jnp.float32),
            jax.ShapeDtypeStruct((chans, wide), jnp.float32),
        ),
        in_specs=[smem] * 3 + [vmem] * 9,
        out_specs=(vmem,) * 5,
        scratch_shapes=[
            pltpu.VMEM((all_rows + 2 * edge, chans, width), jnp.bfloat16),
            pltpu.VMEM((all_rows + 2 * edge, 8, width), jnp.float32),
            pltpu.VMEM((3, chans, width), jnp.float32),
            pltpu.VMEM((all_rows, 3 * chans, width), jnp.bfloat16),
            pltpu.VMEM((all_rows + 2 * edge, chans, width), jnp.float32),
            pltpu.VMEM((all_rows, chans, width), jnp.float32),
            pltpu.VMEM((all_rows, chans, width), jnp.bfloat16),
        ],
        compiler_params=pltpu.CompilerParams(vmem_limit_bytes=60 * 1024 * 1024),
        cost_estimate=pl.CostEstimate(flops=4000000000, bytes_accessed=2000000, transcendentals=0),
        name="band",
    )(dil, place, denom, near, far, fmask, lanes, limits, target, head, wfwd, wback)


def shards(
    encoder_in,
    gain_enc,
    conv_one,
    proj_weight,
    conv_two,
    head_weight,
    target,
    valid_bins,
    offset_limit,
    dilations,
):
    chans, encoder_bins = encoder_in.shape
    width_in = conv_one.shape[2]
    second_channels = conv_two.shape[1]
    tile_rows, tile_cols = target.shape
    first_dilation = dilations[0]
    second_dilation = dilations[1]
    activ = jax.nn.gelu(gain_enc[:, None] * encoder_in.astype(jnp.float32)).astype(jnp.bfloat16)
    framed = with_halo(activ, (("enc", 1),), LARGEST_DILATION)
    channel_count = lax.all_gather(framed, ("bin", "off"), axis=0, tiled=True)
    stacked_enc = jnp.concatenate(
        [
            lax.dynamic_slice_in_dim(
                channel_count,
                LARGEST_DILATION + (kernel_tap_index - 1) * first_dilation,
                encoder_bins,
                1,
            )
            for kernel_tap_index in range(3)
        ],
        axis=0,
    )
    weight_one = jnp.transpose(conv_one, (1, 0, 2)).reshape(chans, 3 * width_in)
    conv_out = jnp.dot(weight_one, stacked_enc, preferred_element_type=jnp.float32)
    hidden = (encoder_in.astype(jnp.float32) + conv_out).astype(jnp.bfloat16)
    proj_rows = jnp.transpose(proj_weight, (0, 2, 1)).reshape(2 * second_channels, chans)
    partial_embed = jnp.dot(proj_rows, hidden, preferred_element_type=jnp.float32)
    summed = lax.psum(partial_embed, ("bin", "off")).astype(jnp.bfloat16)
    embed = lax.all_gather(summed, "enc", axis=1, tiled=True)
    sequence_length = embed.shape[1]
    window_extent = tile_cols * lax.axis_size("enc") * lax.axis_size("off")
    row_start = lax.axis_index("bin") * tile_rows
    offs_start = (lax.axis_index("enc") * lax.axis_size("off") + lax.axis_index("off")) * tile_cols
    edge = LARGEST_DILATION
    width = round_up(tile_rows + 4 * edge, 128)
    wide = round_up(tile_rows + tile_cols + 10 * edge, 128)
    bin_ids = row_start - 2 * edge + jnp.arange(width, dtype=jnp.int32)
    inside = (bin_ids >= 0) & (bin_ids < sequence_length)
    near = lax.dynamic_slice_in_dim(
        jnp.pad(embed[:second_channels].astype(jnp.float32), ((0, 0), (2 * edge, width))),
        row_start,
        width,
        1,
    )
    near = jnp.where(inside[None, :], near, -jnp.inf)
    far = lax.dynamic_slice_in_dim(
        jnp.pad(
            embed[second_channels:].astype(jnp.float32), ((0, 0), (5 * edge, window_extent + wide))
        ),
        row_start + offs_start,
        wide,
        1,
    )
    mask_float = valid_bins.astype(jnp.float32)
    far_mask = lax.dynamic_slice_in_dim(
        jnp.pad(mask_float, (5 * edge, window_extent + wide)), row_start + offs_start, wide
    )
    near_mask = lax.dynamic_slice_in_dim(
        jnp.pad(mask_float, (2 * edge, width)), row_start, width
    )
    limits = lax.dynamic_slice_in_dim(jnp.pad(offset_limit, (2 * edge, width)), row_start, width)
    spots = jnp.arange(width, dtype=jnp.int32)
    framed_lane = (spots >= edge) & (spots < tile_rows + 3 * edge)
    own_lane = (spots >= 2 * edge) & (spots < tile_rows + 2 * edge)
    lanes = jnp.stack([jnp.where(framed_lane, near_mask, 0.0), own_lane.astype(jnp.float32)])
    lanes = jnp.pad(lanes, ((0, 6), (0, 0)))
    denom = 1.0 + count_cells(valid_bins, offset_limit)
    framed_target = with_halo(target, (("bin", 0), (("enc", "off"), 1)), edge)
    target_rows = jnp.pad(
        framed_target.T.astype(jnp.float32), ((0, 0), (edge, width - tile_rows - 3 * edge))
    )
    taps = conv_two.reshape(3, 3, second_channels, second_channels)
    weight_fwd = jnp.transpose(taps, (1, 3, 0, 2)).reshape(3 * second_channels, 3 * second_channels)
    weight_back = jnp.transpose(taps, (1, 2, 0, 3)).reshape(3 * second_channels, 3 * second_channels)
    pred_rows, error_lanes, grad_taps, near_lanes, far_lanes = band(
        near,
        far,
        jnp.broadcast_to(far_mask[None, :], (8, wide)),
        lanes,
        limits[None, :],
        target_rows,
        jnp.broadcast_to(head_weight[:, None], (second_channels, width)),
        weight_fwd,
        weight_back,
        second_dilation.reshape(1),
        jnp.stack([offs_start, jnp.full((), window_extent, jnp.int32)]).astype(jnp.int32),
        denom.reshape(1),
        tile_cols,
    )
    prediction = pred_rows[edge : edge + tile_cols, 2 * edge : 2 * edge + tile_rows].T
    error_sum = jnp.sum(error_lanes)
    grad_band = jnp.transpose(
        grad_taps.reshape(3, second_channels, 3, second_channels), (0, 2, 1, 3)
    ).reshape(9, second_channels, second_channels)
    near_grad = near_lanes[:, 2 * edge : 2 * edge + tile_rows]
    far_grad = far_lanes[:, 5 * edge : 5 * edge + tile_rows + tile_cols - 1]
    enc_start = lax.axis_index("enc") * encoder_bins
    buffer = jnp.zeros((2, second_channels, sequence_length + window_extent), jnp.float32)
    buffer = lax.dynamic_update_slice(buffer, near_grad[None], (0, 0, row_start))
    buffer = lax.dynamic_update_slice(buffer, far_grad[None], (1, 0, row_start + offs_start))
    buffer = buffer[:, :, :sequence_length]
    grad_whole, grad_conv_two, total_error = lax.psum(
        (buffer, grad_band, error_sum), ("enc", "bin", "off")
    )
    grad_embed = lax.dynamic_slice_in_dim(grad_whole, enc_start, encoder_bins, 2).astype(
        jnp.bfloat16
    )
    grad_rows = grad_embed.reshape(2 * second_channels, encoder_bins)
    dhidden = jnp.dot(proj_rows.T, grad_rows, preferred_element_type=jnp.float32).astype(
        jnp.bfloat16
    )
    proj_local = jnp.dot(hidden, grad_rows.T, preferred_element_type=jnp.float32)
    proj_local = jnp.transpose(proj_local.reshape(chans, 2, second_channels), (1, 0, 2))
    conv_local = lax.dot_general(
        dhidden, stacked_enc, (((1,), (1,)), ((), ())), preferred_element_type=jnp.float32
    )
    conv_local = jnp.transpose(conv_local.reshape(chans, 3, width_in), (1, 0, 2))
    grad_proj = lax.psum(proj_local, "enc")
    grad_conv_one = lax.psum_scatter(conv_local, "enc", scatter_dimension=2, tiled=True)
    loss_mean = (total_error / denom).reshape(1)
    return (prediction, loss_mean, grad_conv_two, grad_proj, grad_conv_one)


def solution(mesh):
    in_specs = (
        P(("bin", "off"), "enc"),
        P(("bin", "off")),
        P(None, ("bin", "off"), None),
        P(None, ("bin", "off"), None),
        P(),
        P(),
        P("bin", ("enc", "off")),
        P(),
        P(),
        P(),
    )
    out_specs = (
        P("bin", ("enc", "off")),
        P(),
        P(),
        P(None, ("bin", "off"), None),
        P(None, ("bin", "off"), "enc"),
    )
    return jax.shard_map(shards, mesh=mesh, in_specs=in_specs, out_specs=out_specs, check_vma=False)
```

time: 684 us -> 282 us (0.41); the launches traced: 674 us -> 281 us
  local copies, waits for them, and re-layouts: 407 us -> 53.6 us
  Pallas kernels: 0 us -> 52.2 us
  other arithmetic: 50.8 us -> 11 us
  matrix products: 39.1 us -> 1.2 us
  starting transfers between devices: 28.9 us -> 14.6 us
    unnamed x93 -> x14, local copies, waits for them, and re-layouts: 145 us -> 39.7 us
    dynamic_slice x5 -> x2, local copies, waits for them, and re-layouts: 74.4 us -> 1.46 us  [the longest x1 1.38 us: shards(): lax.dynamic_slice_in_dim(jnp.pad(offset_limit, (2 * edge, width)), row_st...]
    reshape x4 -> x5, local copies, waits for them, and re-layouts: 70.6 us -> 4.3 us  [the longest x2 1.94 us: shards(): taps = conv_two.reshape(3, 3, second_channels, second_channels)]
    pallas_call x0 -> x1, Pallas kernels: none -> 52.2 us  [band(): pl.pallas_call(functools.partial(band_body, edge, rows, 4), out_shape=(ja...]
    dot_general x3 -> x0, matrix products: 37.9 us -> none  [the longest x1 14.4 us: shards(): lax.dot_general(stacked_band, dres.reshape(second_channels, area), (((1,)...]
    pad x3 -> x0, local copies, waits for them, and re-layouts: 30.5 us -> none  [the longest x2 16.1 us: hankel(): tiled = jnp.pad(tiled, ((0, 0), (0, tile_rows)))]
    concatenate x5 -> x1, other arithmetic: 18.4 us -> 0.09 us  [with_halo(): jnp.concatenate([lax.ppermute(tail, axis, [(i, (i + 1) % count) for i in...]
    reduce_sum x4 -> x2, other arithmetic: 21.8 us -> 4.85 us  [the longest x1 3.57 us: count_cells(): inside = jnp.sum(jnp.where(scored, valid_bins[None, :], 0), axis=1)]
  transfers between devices with their start and end apart: 11 -> 7, of which waited for: 2 -> 1; matrix products, arithmetic and copies ran while one was open for 11% -> 7% of each run, Pallas kernels for 0% -> 0%
where the time goes in v1:
time: 282 us; the launch traced here: 281 us
  blocking collectives  126 us (45%)
  local copies, waits for them, and re-layouts  53.6 us (19%)
  Pallas kernels  52.2 us (19%)
  between operations  18.7 us (7%)
  starting transfers between devices  14.6 us (5%)
  other arithmetic  11 us (4%)
  waiting for transfers between devices  3.9 us (1%)
    pallas_call x1, Pallas kernels, band(): pl.pallas_call(functools.partial(band_body, edge, rows, 4), out_shape=(ja...  52.2 us
    psum x1, blocking collectives, shards(): lax.psum((buffer, grad_band, error_sum), ('enc', 'bin', 'off'))  49.2 us
    unnamed x14, local copies, waits for them, and re-layouts  39.7 us
    psum x1, blocking collectives, shards(): summed = lax.psum(partial_embed, ('bin', 'off')).astype(jnp.bfloat16)  25.3 us
    psum x1, blocking collectives, shards(): grad_proj = lax.psum(proj_local, 'enc')  18.8 us
    all_gather x1, blocking collectives, shards(): channel_count = lax.all_gather(framed, ('bin', 'off'), axis=0, tiled=True)  17.4 us
    all_gather x1, blocking collectives, shards(): embed = lax.all_gather(summed, 'enc', axis=1, tiled=True)  15 us
    ppermute x3, starting transfers between devices, with_halo(): lax.ppermute(tail, axis, [(i, (i + 1) % count) for i in range(ends)])  10.7 us
  transfers between devices with their start and end apart: 7, of which 1 were waited for; matrix products, arithmetic and copies ran while one was open for 7% of the time, Pallas kernels for 0%

profile of v1, /device:TPU:0, one launch (start us, length us, event | category | flops | bytes accessed | tf_op | source)
XLA Modules:
  0.0 280.9 jit_solution(8431496066416951066)
XLA Ops:
  8.1 1.3 collective-permute-start.3
  9.5 3.0 %collective-permute-start.2 = (bf16[8,128]{0,1:T(8,128)(2,1)S(1)}, bf16[8,128]{0,1:T(8,128)(2,1)S(1)}, u32[]{:S(2)}, u32[]{:S(2)}) collective-permute-start(bf16[8,128]{0,1:T(8,128)(2,1)S(1)} %copy.50), channel_id=1, source_target_pairs={{0,2},{2,4},{4,6},{1,3},{3,5},{5,7},{8,10},{10,12},{12,14},{9,11},... | collective-permute-start | bytes 6152 | tf_op jit(solution)/shard_map/ppermute | solution.py:21
  12.5 0.9 fusion.9
  13.5 4.9 %collective-permute-start = (bf16[64,8]{1,0:T(8,128)(2,1)S(1)}, bf16[64,8]{1,0:T(8,128)(2,1)S(1)}, u32[]{:S(2)}, u32[]{:S(2)}) collective-permute-start(bf16[64,8]{1,0:T(8,128)(2,1)S(1)} %get-tuple-element.52), channel_id=1, source_target_pairs={{0,8},{8,16},{16,24},{1,9},{9,17},{17,25},{2,10},{10,18},{18,26},{... | collective-permute-start | bytes 3080 | tf_op jit(solution)/shard_map/ppermute | solution.py:21
  18.4 1.3 collective-permute-start.1
  19.7 1.4 fusion.33
  23.1 1.0 copy.52
  24.1 0.9 copy.63
  25.0 1.0 copy.53
  26.1 1.4 pad_dynamic-slice_fusion.3
  27.4 3.6 %select_reduce_fusion = s32[1536]{0:T(1024)S(1)} fusion(s32[1536]{0:T(1024)} %param.17, s32[1536]{0:T(1024)} %param.18), kind=kLoop, calls=%fused_computation | loop fusion | flops 14154240 | bytes 18432 | tf_op jit(solution)/shard_map/reduce_sum | solution.py:35
  31.0 1.4 fusion.32
  35.9 0.9 copy.61
  36.9 17.4 %all_gather.6 = bf16[512,400]{1,0:T(8,128)(2,1)S(1)} all-gather(bf16[64,400]{1,0:T(8,128)(2,1)S(1)} %pad_maximum_fusion.3), channel_id=1, replica_groups=mesh['enc'=4,'bin'=4,'off'=2] {'bin','off'}, dimensions={0}, use_global_device_ids=true | all-gather | bytes 460800 | tf_op jit(solution)/shard_map/all_gather | solution.py:238
  55.4 25.3 %psum.35 = bf16[64,384]{1,0:T(8,128)(2,1)S(1)} all-reduce(f32[64,384]{1,0:T(8,128)S(1)} %convolution_bitcast_fusion.1), channel_id=1, replica_groups=mesh['enc'=4,'bin'=4,'off'=2] {'bin','off'}, use_global_device_ids=true, to_apply=%region_2.3 | all-reduce | flops 24576 | bytes 147456 | tf_op jit(solution)/shard_map/psum | solution.py:256
  80.6 15.0 %all_gather.7 = bf16[64,1536]{1,0:T(8,128)(2,1)S(1)} all-gather(bf16[64,384]{1,0:T(8,128)(2,1)S(1)} %psum.35), channel_id=1, replica_groups=mesh['enc'=4,'bin'=4,'off'=2] {'enc'}, dimensions={1}, use_global_device_ids=true | all-gather | bytes 245760 | tf_op jit(solution)/shard_map/all_gather | solution.py:257
  96.4 2.8 collective-permute-start.4
  99.2 1.3 collective-permute-start.5
  101.2 3.9 %collective-permute-done.5 = bf16[400,8]{0,1:T(8,128)(2,1)S(1)} collective-permute-done((bf16[400,8]{0,1:T(8,128)(2,1)S(1)}, bf16[400,8]{0,1:T(8,128)(2,1)S(1)}, u32[]{:S(2)}, u32[]{:S(2)}) %collective-permute-start.5) | collective-permute-done | bytes 6432 | tf_op jit(solution)/shard_map/ppermute | solution.py:23
  105.2 0.8 pad_convert_fusion.target_ref
  107.4 52.2 %band.1 = (f32[144,512]{1,0:T(8,128)}, f32[1,512]{1,0:T(1,128)}, f32[96,96]{1,0:T(8,128)}, f32[32,512]{1,0:T(8,128)}, f32[32,640]{1,0:T(8,128)}) custom-call(s32[1]{0:T(128)} %get-tuple-element.57.dil_ref, s32[2]{0:T(128)} %pad_add_fusion.place_ref, f32[1]{0:T(128)} %bitcast.1.denom_ref, f32[32,512]{1,0:T(8,128)} %convert_select_fusion.near_ref, ...), custom_call_target="tpu_custom_call" | custom-call | flops 4000000000 | bytes 2000000 | tf_op jit(solution)/shard_map/band/pallas_call | solution.py:192
  159.6 1.0 slice_bitcast_fusion.1
  160.5 0.9 reshape.92
  161.5 1.3 reduce_sum.29
  162.8 0.9 bitcast_dynamic-update-slice_fusion
  164.4 49.2 %all-reduce.9 = (f32[]{:T(128)}, f32[9,32,32]{2,1,0:T(8,128)}, bf16[2,32,1536]{2,1,0:T(8,128)(2,1)S(1)}) all-reduce(f32[]{:T(128)} %reduce_sum.29, f32[9,32,32]{2,1,0:T(8,128)S(1)} %bitcast.64, f32[2,32,1536]{2,1,0:T(8,128)S(1)} %slice.60), channel_id=1, replica_groups=mesh['enc'=4,'bin'=4,'off'=2] {'enc','bin','off'}, use_global_device_ids=true, to_apply=%region_4.5 | all-reduce | flops 107521 | bytes 663560 | tf_op jit(solution)/shard_map/psum | solution.py:330
  214.5 13.8 %copy.58 = f32[3,64,512]{0,1,2:T(8,128)} copy(f32[3,64,512]{2,0,1:T(4,128)S(1)} %bitcast.62) | data formatting | bytes 786432
  228.2 13.3 %reshape.97 = f32[512,192]{1,0:T(8,128)} reshape(f32[512,64,3]{2,1,0:T(8,128)} %bitcast.60) | data formatting | bytes 786432
  241.7 0.8 copy.56
  243.3 18.8 %psum.39 = f32[2,64,32]{1,2,0:T(8,128)} all-reduce(f32[2,64,32]{1,2,0:T(8,128)S(1)} %convolution_bitcast_fusion.3), channel_id=1, replica_groups=mesh['enc'=4,'bin'=4,'off'=2] {'enc'}, use_global_device_ids=true, to_apply=%region_7.8 | all-reduce | flops 4096 | bytes 32768 | tf_op jit(solution)/shard_map/psum | solution.py:346
  262.1 6.4 %reshape.98 = f32[128,64,3]{2,1,0:T(8,128)} reshape(f32[128,192]{1,0:T(8,128)} %reduce-scatter.4.cloned.1.call-done) | data formatting | bytes 196608
  268.5 4.4 %copy.57 = f32[3,64,128]{2,1,0:T(8,128)} copy(f32[3,64,128]{0,1,2:T(8,128)} %bitcast.61) | data formatting | bytes 196608
  (47 shorter events, 9.8 us)
Async XLA Ops:
  7.2 48.0 %copy-start = (bf16[2,64,32]{1,2,0:T(8,128)(2,1)S(1)}, bf16[2,64,32]{1,2,0:T(8,128)(2,1)}, u32[]{:S(2)}) copy-start(bf16[2,64,32]{1,2,0:T(8,128)(2,1)} %param.13) | copy-start | bytes 24580
  7.2 255.0 %reduce-scatter.4.cloned.1.call-start = ((), (), s32[]{:S(2)}) async-start(), calls=%async_computation.1 | async-start | bytes 655360
  8.1 88.3 %collective-permute-start.3 = (bf16[8,128]{0,1:T(8,128)(2,1)S(1)}, bf16[8,128]{0,1:T(8,128)(2,1)S(1)}, u32[]{:S(2)}, u32[]{:S(2)}) collective-permute-start(bf16[8,128]{0,1:T(8,128)(2,1)S(1)} %copy.51), channel_id=1, source_target_pairs={{2,0},{4,2},{6,4},{3,1},{5,3},{7,5},{10,8},{12,10},{14,12},{11,9},... | collective-permute-start | bytes 6152 | tf_op jit(solution)/shard_map/ppermute | solution.py:23
  9.3 45.5 %copy-start.2 = (bf16[64,384]{1,0:T(8,128)(2,1)S(1)}, bf16[64,384]{1,0:T(8,128)(2,1)}, u32[]{:S(2)}) copy-start(bf16[64,384]{1,0:T(8,128)(2,1)} %param.10) | copy-start | bytes 147460
  9.5 86.9 %collective-permute-start.2 = (bf16[8,128]{0,1:T(8,128)(2,1)S(1)}, bf16[8,128]{0,1:T(8,128)(2,1)S(1)}, u32[]{:S(2)}, u32[]{:S(2)}) collective-permute-start(bf16[8,128]{0,1:T(8,128)(2,1)S(1)} %copy.50), channel_id=1, source_target_pairs={{0,2},{2,4},{4,6},{1,3},{3,5},{5,7},{8,10},{10,12},{12,14},{9,11},... | collective-permute-start | bytes 6152 | tf_op jit(solution)/shard_map/ppermute | solution.py:21
  13.5 23.3 %collective-permute-start = (bf16[64,8]{1,0:T(8,128)(2,1)S(1)}, bf16[64,8]{1,0:T(8,128)(2,1)S(1)}, u32[]{:S(2)}, u32[]{:S(2)}) collective-permute-start(bf16[64,8]{1,0:T(8,128)(2,1)S(1)} %get-tuple-element.52), channel_id=1, source_target_pairs={{0,8},{8,16},{16,24},{1,9},{9,17},{17,25},{2,10},{10,18},{18,26},{... | collective-permute-start | bytes 3080 | tf_op jit(solution)/shard_map/ppermute | solution.py:21
  18.4 18.4 %collective-permute-start.1 = (bf16[64,8]{1,0:T(8,128)(2,1)S(1)}, bf16[64,8]{1,0:T(8,128)(2,1)S(1)}, u32[]{:S(2)}, u32[]{:S(2)}) collective-permute-start(bf16[64,8]{1,0:T(8,128)(2,1)S(1)} %get-tuple-element.53), channel_id=1, source_target_pairs={{8,0},{16,8},{24,16},{9,1},{17,9},{25,17},{10,2},{18,10},{26,18},{... | collective-permute-start | bytes 3080 | tf_op jit(solution)/shard_map/ppermute | solution.py:23
  54.9 51.8 %copy-start.3 = (f32[32]{0:T(128)S(1)}, f32[32]{0:T(128)}, u32[]{:S(2)}) copy-start(f32[32]{0:T(128)} %param.15) | copy-start | bytes 388
  96.4 4.8 %collective-permute-start.4 = (bf16[400,8]{0,1:T(8,128)(2,1)S(1)}, bf16[400,8]{0,1:T(8,128)(2,1)S(1)}, u32[]{:S(2)}, u32[]{:S(2)}) collective-permute-start(bf16[400,8]{0,1:T(8,128)(2,1)S(1)} %get-tuple-element.48), channel_id=1, source_target_pairs={{0,1},{1,8},{8,9},{9,16},{16,17},{17,24},{24,25},{2,3},{3,10},{10,... | collective-permute-start | bytes 19208 | tf_op jit(solution)/shard_map/ppermute | solution.py:21
  99.2 5.9 %collective-permute-start.5 = (bf16[400,8]{0,1:T(8,128)(2,1)S(1)}, bf16[400,8]{0,1:T(8,128)(2,1)S(1)}, u32[]{:S(2)}, u32[]{:S(2)}) collective-permute-start(bf16[400,8]{0,1:T(8,128)(2,1)S(1)} %get-tuple-element.49), channel_id=1, source_target_pairs={{1,0},{8,1},{9,8},{16,9},{17,16},{24,17},{25,24},{3,2},{10,3},{11,... | collective-permute-start | bytes 19208 | tf_op jit(solution)/shard_map/ppermute | solution.py:23
  228.2 13.4 %copy-start.1 = (f32[144,512]{1,0:T(8,128)S(1)}, f32[144,512]{1,0:T(8,128)}, u32[]{:S(2)}) copy-start(f32[144,512]{1,0:T(8,128)} %get-tuple-element.10) | copy-start | bytes 884740
Sparse Core Ops, SparseCore 0:
  241.7 20.2 reduce-scatter.3

commit v2 on v1

--- a/solution.py
+++ b/solution.py
@@ -34,6 +34,276 @@
     scored = (gap >= 0) & (gap < offset_limit[:, None])
     inside = jnp.sum(jnp.where(scored, valid_bins[None, :], 0), axis=1)
     return jnp.sum(valid_bins * inside).astype(jnp.float32)
+
+
+def place_of(enc_index, group_index, offs):
+    return (enc_index, group_index // offs, lax.rem(group_index, offs))
+
+
+def each(count, body):
+    def step(index, carry):
+        body(index)
+        return carry
+
+    lax.fori_loop(0, count, step, 0)
+
+
+def push(src, dst, send_sem, recv_sem, where):
+    return pltpu.make_async_remote_copy(
+        src_ref=src,
+        dst_ref=dst,
+        send_sem=send_sem,
+        recv_sem=recv_sem,
+        device_id=where,
+        device_id_type=pl.DeviceIdType.MESH,
+    )
+
+
+def greet(where):
+    pl.semaphore_signal(
+        pltpu.get_barrier_semaphore(), inc=1, device_id=where, device_id_type=pl.DeviceIdType.MESH
+    )
+
+
+def gather_body(encs, bins, offs, x_ref, out_ref, send_group, recv_group, send_edge, recv_edge):
+    group = bins * offs
+    side = 128
+    span = x_ref.shape[1]
+    z = lax.axis_index("enc")
+    g = lax.axis_index("bin") * offs + lax.axis_index("off")
+
+    def peer(k):
+        return lax.rem(g + k + 1, group)
+
+    each(group - 1, lambda k: greet(place_of(z, peer(k), offs)))
+
+    @pl.when(z > 0)
+    def _():
+        each(group, lambda h: greet(place_of(z - 1, h, offs)))
+
+    @pl.when(z < encs - 1)
+    def _():
+        each(group, lambda h: greet(place_of(z + 1, h, offs)))
+
+    sides = jnp.minimum(z, 1) + jnp.minimum(encs - 1 - z, 1)
+    pl.semaphore_wait(pltpu.get_barrier_semaphore(), group - 1 + group * sides)
+
+    def middle(k, owner):
+        return push(
+            x_ref,
+            out_ref.at[owner, :, pl.ds(side, span)],
+            send_group.at[k],
+            recv_group.at[owner],
+            place_of(z, peer(k), offs),
+        )
+
+    def to_left(h, owner):
+        return push(
+            x_ref.at[:, pl.ds(0, side)],
+            out_ref.at[owner, :, pl.ds(side + span, side)],
+            send_edge.at[0, h],
+            recv_edge.at[0, owner],
+            place_of(z - 1, h, offs),
+        )
+
+    def to_right(h, owner):
+        return push(
+            x_ref.at[:, pl.ds(span - side, side)],
+            out_ref.at[owner, :, pl.ds(0, side)],
+            send_edge.at[1, h],
+            recv_edge.at[1, owner],
+            place_of(z + 1, h, offs),
+        )
+
+    each(group - 1, lambda k: middle(k, g).start())
+
+    @pl.when(z > 0)
+    def _():
+        each(group, lambda h: to_left(h, g).start())
+
+    @pl.when(z < encs - 1)
+    def _():
+        each(group, lambda h: to_right(h, g).start())
+
+    out_ref[g, :, side : side + span] = x_ref[...]
+    blank = jnp.zeros((group, x_ref.shape[0], side), x_ref.dtype)
+
+    @pl.when(z == 0)
+    def _():
+        out_ref[:, :, :side] = blank
+
+    @pl.when(z == encs - 1)
+    def _():
+        out_ref[:, :, side + span :] = blank
+
+    def settle(k):
+        middle(k, g).wait_send()
+        middle(k, peer(k)).wait_recv()
+
+    each(group - 1, settle)
+
+    @pl.when(z > 0)
+    def _():
+        def settle_left(h):
+            to_left(h, g).wait_send()
+            to_right(h, h).wait_recv()
+
+        each(group, settle_left)
+
+    @pl.when(z < encs - 1)
+    def _():
+        def settle_right(h):
+            to_right(h, g).wait_send()
+            to_left(h, h).wait_recv()
+
+        each(group, settle_right)
+
+
+def gather_framed(x, encs, bins, offs):
+    group = bins * offs
+    vmem = pl.BlockSpec(memory_space=pltpu.VMEM)
+    return pl.pallas_call(
+        functools.partial(gather_body, encs, bins, offs),
+        out_shape=jax.ShapeDtypeStruct((group, x.shape[0], x.shape[1] + 256), x.dtype),
+        in_specs=[vmem],
+        out_specs=vmem,
+        scratch_shapes=[
+            pltpu.SemaphoreType.DMA((group,)),
+            pltpu.SemaphoreType.DMA((group,)),
+            pltpu.SemaphoreType.DMA((2, group)),
+            pltpu.SemaphoreType.DMA((2, group)),
+        ],
+        compiler_params=pltpu.CompilerParams(collective_id=0, has_side_effects=True),
+        name="gather_framed",
+    )(x)
+
+
+def exchange_body(
+    encs, bins, offs, spread, x_ref, out_ref, slots, total, lines, sends, recvs, line_sends, line_recvs
+):
+    group = bins * offs
+    z = lax.axis_index("enc")
+    g = lax.axis_index("bin") * offs + lax.axis_index("off")
+
+    def peer(k):
+        return lax.rem(g + k + 1, group)
+
+    def line(k):
+        return lax.rem(z + k + 1, encs)
+
+    def in_group(k):
+        return place_of(z, peer(k), offs)
+
+    def in_line(k):
+        return place_of(line(k), g, offs)
+
+    each(group - 1, lambda k: greet(in_group(k)))
+    each(encs - 1, lambda k: greet(in_line(k)))
+    pl.semaphore_wait(pltpu.get_barrier_semaphore(), group + encs - 2)
+
+    def split(k, owner):
+        return push(
+            x_ref.at[peer(k)], slots.at[owner], sends.at[0, k], recvs.at[0, owner], in_group(k)
+        )
+
+    each(group - 1, lambda k: split(k, g).start())
+    slots[g] = x_ref[g]
+
+    def settle_split(k):
+        split(k, g).wait_send()
+        split(k, peer(k)).wait_recv()
+
+    each(group - 1, settle_split)
+    summed = slots[0]
+    for h in range(1, group):
+        summed = summed + slots[h]
+    if spread:
+        total[...] = summed
+
+        def across(k, owner, part):
+            return push(
+                total.at[encs if part else line(k)],
+                lines.at[owner, part],
+                line_sends.at[part, k],
+                line_recvs.at[part, owner],
+                in_line(k),
+            )
+
+        def begin_across(k):
+            for part in range(2):
+                across(k, z, part).start()
+
+        each(encs - 1, begin_across)
+        lines[z, 0] = total[z]
+        lines[z, 1] = total[encs]
+
+        def settle_across(k):
+            for part in range(2):
+                across(k, z, part).wait_send()
+                across(k, line(k), part).wait_recv()
+
+        each(encs - 1, settle_across)
+        piece = lines[0, 0]
+        shared = lines[0, 1]
+        for other in range(1, encs):
+            piece = piece + lines[other, 0]
+            shared = shared + lines[other, 1]
+        out_ref[g, encs] = shared
+    else:
+        piece = summed[0]
+    out_ref[g, z] = piece.astype(jnp.bfloat16).astype(jnp.float32)
+
+    def along(k, owner):
+        return push(
+            out_ref.at[g, z],
+            out_ref.at[g, owner],
+            line_sends.at[2, k],
+            line_recvs.at[2, owner],
+            in_line(k),
+        )
+
+    each(encs - 1, lambda k: along(k, z).start())
+
+    def settle_along(k):
+        along(k, z).wait_send()
+        along(k, line(k)).wait_recv()
+
+    each(encs - 1, settle_along)
+
+    def spread_out(k, owner):
+        return push(
+            out_ref.at[g], out_ref.at[owner], sends.at[1, k], recvs.at[1, owner], in_group(k)
+        )
+
+    each(group - 1, lambda k: spread_out(k, g).start())
+
+    def settle_out(k):
+        spread_out(k, g).wait_send()
+        spread_out(k, peer(k)).wait_recv()
+
+    each(group - 1, settle_out)
+
+
+def exchange(x, encs, bins, offs, spread, ident, name):
+    group, parts, rows, span = x.shape
+    vmem = pl.BlockSpec(memory_space=pltpu.VMEM)
+    return pl.pallas_call(
+        functools.partial(exchange_body, encs, bins, offs, spread),
+        out_shape=jax.ShapeDtypeStruct((group, encs + int(spread), rows, span), jnp.float32),
+        in_specs=[vmem],
+        out_specs=vmem,
+        scratch_shapes=[
+            pltpu.VMEM((group, parts, rows, span), jnp.float32),
+            pltpu.VMEM((parts, rows, span), jnp.float32),
+            pltpu.VMEM((encs, 2, rows, span), jnp.float32),
+            pltpu.SemaphoreType.DMA((2, group)),
+            pltpu.SemaphoreType.DMA((2, group)),
+            pltpu.SemaphoreType.DMA((3, encs)),
+            pltpu.SemaphoreType.DMA((3, encs)),
+        ],
+        compiler_params=pltpu.CompilerParams(collective_id=ident, has_side_effects=True),
+        name=name,
+    )(x)
 
 
 def round_up(value, step):
@@ -234,17 +504,14 @@
     first_dilation = dilations[0]
     second_dilation = dilations[1]
     activ = jax.nn.gelu(gain_enc[:, None] * encoder_in.astype(jnp.float32)).astype(jnp.bfloat16)
-    framed = with_halo(activ, (("enc", 1),), LARGEST_DILATION)
-    channel_count = lax.all_gather(framed, ("bin", "off"), axis=0, tiled=True)
+    encs, bins, offs = (lax.axis_size(axis) for axis in ("enc", "bin", "off"))
+    group = bins * offs
+    rows_piece = 2 * second_channels // group
+    framed = gather_framed(activ, encs, bins, offs).reshape(width_in, encoder_bins + 256)
     stacked_enc = jnp.concatenate(
         [
-            lax.dynamic_slice_in_dim(
-                channel_count,
-                LARGEST_DILATION + (kernel_tap_index - 1) * first_dilation,
-                encoder_bins,
-                1,
-            )
-            for kernel_tap_index in range(3)
+            lax.dynamic_slice_in_dim(framed, 128 + (tap - 1) * first_dilation, encoder_bins, 1)
+            for tap in range(3)
         ],
         axis=0,
     )
@@ -253,10 +520,31 @@
     hidden = (encoder_in.astype(jnp.float32) + conv_out).astype(jnp.bfloat16)
     proj_rows = jnp.transpose(proj_weight, (0, 2, 1)).reshape(2 * second_channels, chans)
     partial_embed = jnp.dot(proj_rows, hidden, preferred_element_type=jnp.float32)
-    summed = lax.psum(partial_embed, ("bin", "off")).astype(jnp.bfloat16)
-    embed = lax.all_gather(summed, "enc", axis=1, tiled=True)
+    pieces = exchange(
+        partial_embed.reshape(group, 1, rows_piece, encoder_bins), encs, bins, offs, False, 1, "embed"
+    )
+    embed = jnp.transpose(pieces, (0, 2, 1, 3)).reshape(2 * second_channels, encs * encoder_bins)
+    enc_index = lax.axis_index("enc")
+    share = width_in // encs
+
+    def parcel(owner):
+        rows = lax.dynamic_slice(framed, (owner * share, 128), (share, encoder_bins))
+        return jnp.concatenate([rows, hidden], axis=0)
+
+    whole_side = jnp.zeros((share + chans, encs * encoder_bins), jnp.bfloat16)
+    whole_side = lax.dynamic_update_slice(
+        whole_side, parcel(enc_index), (0, enc_index * encoder_bins)
+    )
+    for hop in range(1, encs):
+        arrived = lax.ppermute(
+            parcel(lax.rem(enc_index + hop, encs)),
+            "enc",
+            [(i, (i + hop) % encs) for i in range(encs)],
+        )
+        origin = lax.rem(enc_index + encs - hop, encs)
+        whole_side = lax.dynamic_update_slice(whole_side, arrived, (0, origin * encoder_bins))
     sequence_length = embed.shape[1]
-    window_extent = tile_cols * lax.axis_size("enc") * lax.axis_size("off")
+    window_extent = tile_cols * encs * offs
     row_start = lax.axis_index("bin") * tile_rows
     offs_start = (lax.axis_index("enc") * lax.axis_size("off") + lax.axis_index("off")) * tile_cols
     edge = LARGEST_DILATION
@@ -265,7 +553,7 @@
     bin_ids = row_start - 2 * edge + jnp.arange(width, dtype=jnp.int32)
     inside = (bin_ids >= 0) & (bin_ids < sequence_length)
     near = lax.dynamic_slice_in_dim(
-        jnp.pad(embed[:second_channels].astype(jnp.float32), ((0, 0), (2 * edge, width))),
+        jnp.pad(embed[:second_channels], ((0, 0), (2 * edge, width))),
         row_start,
         width,
         1,
@@ -273,7 +561,7 @@
     near = jnp.where(inside[None, :], near, -jnp.inf)
     far = lax.dynamic_slice_in_dim(
         jnp.pad(
-            embed[second_channels:].astype(jnp.float32), ((0, 0), (5 * edge, window_extent + wide))
+            embed[second_channels:], ((0, 0), (5 * edge, window_extent + wide))
         ),
         row_start + offs_start,
         wide,
@@ -316,35 +604,57 @@
         tile_cols,
     )
     prediction = pred_rows[edge : edge + tile_cols, 2 * edge : 2 * edge + tile_rows].T
-    error_sum = jnp.sum(error_lanes)
-    grad_band = jnp.transpose(
-        grad_taps.reshape(3, second_channels, 3, second_channels), (0, 2, 1, 3)
-    ).reshape(9, second_channels, second_channels)
     near_grad = near_lanes[:, 2 * edge : 2 * edge + tile_rows]
     far_grad = far_lanes[:, 5 * edge : 5 * edge + tile_rows + tile_cols - 1]
-    enc_start = lax.axis_index("enc") * encoder_bins
-    buffer = jnp.zeros((2, second_channels, sequence_length + window_extent), jnp.float32)
-    buffer = lax.dynamic_update_slice(buffer, near_grad[None], (0, 0, row_start))
-    buffer = lax.dynamic_update_slice(buffer, far_grad[None], (1, 0, row_start + offs_start))
-    buffer = buffer[:, :, :sequence_length]
-    grad_whole, grad_conv_two, total_error = lax.psum(
-        (buffer, grad_band, error_sum), ("enc", "bin", "off")
-    )
-    grad_embed = lax.dynamic_slice_in_dim(grad_whole, enc_start, encoder_bins, 2).astype(
-        jnp.bfloat16
-    )
-    grad_rows = grad_embed.reshape(2 * second_channels, encoder_bins)
+    buffer = jnp.zeros((2 * second_channels, sequence_length + window_extent), jnp.float32)
+    buffer = lax.dynamic_update_slice(buffer, near_grad, (0, row_start))
+    buffer = lax.dynamic_update_slice(buffer, far_grad, (second_channels, row_start + offs_start))
+    buffer = buffer[:, :sequence_length].reshape(group, rows_piece, encs, encoder_bins)
+    taps_rows, error_rows = grad_taps.shape[0], width // 128
+    half = 2 * second_channels
+    common = jnp.concatenate(
+        [
+            jnp.pad(grad_taps, ((0, 0), (0, 128 - taps_rows))),
+            error_lanes.reshape(error_rows, 128),
+            jnp.zeros((2 * half - taps_rows - error_rows, 128), jnp.float32),
+        ]
+    )
+    common = jnp.transpose(common.reshape(group, 2, rows_piece, 128), (0, 2, 1, 3))
+    common = common.reshape(group, 1, rows_piece, 256)
+    common = jnp.pad(common, ((0, 0), (0, 0), (0, 0), (0, encoder_bins - 256)))
+    outgoing = jnp.concatenate([jnp.transpose(buffer, (0, 2, 1, 3)), common], axis=1)
+    summed = exchange(outgoing, encs, bins, offs, True, 2, "grads")
+    grad_rows = jnp.transpose(summed[:, :encs], (0, 2, 1, 3)).reshape(half, sequence_length)
+    grad_rows = grad_rows.astype(jnp.bfloat16)
+    common = summed[:, encs, :, :256].reshape(group, rows_piece, 2, 128)
+    common = jnp.transpose(common, (0, 2, 1, 3)).reshape(2 * half, 128)
+    grad_conv_two = jnp.transpose(
+        common[:taps_rows, :taps_rows].reshape(3, second_channels, 3, second_channels), (0, 2, 1, 3)
+    ).reshape(9, second_channels, second_channels)
+    total_error = jnp.sum(common[taps_rows : taps_rows + error_rows])
     dhidden = jnp.dot(proj_rows.T, grad_rows, preferred_element_type=jnp.float32).astype(
         jnp.bfloat16
     )
-    proj_local = jnp.dot(hidden, grad_rows.T, preferred_element_type=jnp.float32)
-    proj_local = jnp.transpose(proj_local.reshape(chans, 2, second_channels), (1, 0, 2))
-    conv_local = lax.dot_general(
-        dhidden, stacked_enc, (((1,), (1,)), ((), ())), preferred_element_type=jnp.float32
-    )
-    conv_local = jnp.transpose(conv_local.reshape(chans, 3, width_in), (1, 0, 2))
-    grad_proj = lax.psum(proj_local, "enc")
-    grad_conv_one = lax.psum_scatter(conv_local, "enc", scatter_dimension=2, tiled=True)
+    activ_side = jnp.pad(whole_side[:share], ((0, 0), (edge, edge)))
+    hidden_side = whole_side[share:]
+    across = (((1,), (1,)), ((), ()))
+    grad_proj = lax.dot_general(
+        hidden_side, grad_rows, across, preferred_element_type=jnp.float32
+    )
+    grad_proj = jnp.stack([grad_proj[:, :second_channels], grad_proj[:, second_channels:]])
+    grad_conv_one = jnp.stack(
+        [
+            lax.dot_general(
+                dhidden,
+                lax.dynamic_slice_in_dim(
+                    activ_side, edge + (tap - 1) * first_dilation, sequence_length, 1
+                ),
+                across,
+                preferred_element_type=jnp.float32,
+            )
+            for tap in range(3)
+        ]
+    )
     loss_mean = (total_error / denom).reshape(1)
     return (prediction, loss_mean, grad_conv_two, grad_proj, grad_conv_one)
 

time: 282 us -> 163 us (0.58)
  blocking collectives: 126 us -> 0 us
  Pallas kernels: 52.2 us -> 107 us
  local copies, waits for them, and re-layouts: 53.6 us -> 17.4 us
  between operations: 18.7 us -> 6.81 us
  waiting for transfers between devices: 3.9 us -> 0.02 us
    psum x3 -> x0, blocking collectives: 93.2 us -> none  [the longest x1 49.2 us: shards(): lax.psum((buffer, grad_band, error_sum), ('enc', 'bin', 'off'))]
    pallas_call x0 -> x3, Pallas kernels: none -> 55.2 us  [the longest x2 41 us: exchange(): pl.pallas_call(functools.partial(exchange_body, encs, bins, offs, spread)...]
    unnamed x14 -> x26, local copies, waits for them, and re-layouts: 39.7 us -> 1.75 us
    all_gather x2 -> x0, blocking collectives: 32.4 us -> none  [the longest x1 17.4 us: shards(): channel_count = lax.all_gather(framed, ('bin', 'off'), axis=0, tiled=True)]
    ppermute x0 -> x3, starting transfers between devices: none -> 7.04 us  [shards(): lax.ppermute(parcel(lax.rem(enc_index + hop, encs)), 'enc', [(i, (i + hop...]
    slice x2 -> x7, local copies, waits for them, and re-layouts: 0.04 us -> 4.02 us  [the longest x1 1.08 us: shards(): embed[second_channels:]]
    ppermute x3 -> x2, waiting for transfers between devices: 3.88 us -> 0.01 us  [with_halo(): lax.ppermute(head, axis, [((i + 1) % count, i) for i in range(ends)])]
    ppermute x3 -> x2, starting transfers between devices: 10.7 us -> 7.57 us  [with_halo(): lax.ppermute(tail, axis, [(i, (i + 1) % count) for i in range(ends)])]
  transfers between devices with their start and end apart: 7 -> 7, of which waited for: 1 -> 0; matrix products, arithmetic and copies ran while one was open for 7% -> 17% of each run, Pallas kernels for 0% -> 66%
where the time goes in v2:
time: 163 us; the launch traced here: 162 us
  Pallas kernels  107 us (66%)
  local copies, waits for them, and re-layouts  17.4 us (11%)
  starting transfers between devices  17.2 us (11%)
  other arithmetic  11 us (7%)
  between operations  6.81 us (4%)
  matrix products  2.48 us (2%)
    pallas_call x1, Pallas kernels, band(): pl.pallas_call(functools.partial(band_body, edge, rows, 4), out_shape=(ja...  52.1 us
    pallas_call x2, Pallas kernels, exchange(): pl.pallas_call(functools.partial(exchange_body, encs, bins, offs, spread)...  41 us
    pallas_call x1, Pallas kernels, gather_framed(): pl.pallas_call(functools.partial(gather_body, encs, bins, offs), out_shap...  14.1 us
    ppermute x2, starting transfers between devices, with_halo(): lax.ppermute(tail, axis, [(i, (i + 1) % count) for i in range(ends)])  7.57 us
    ppermute x3, starting transfers between devices, shards(): lax.ppermute(parcel(lax.rem(enc_index + hop, encs)), 'enc', [(i, (i + hop...  7.04 us
  transfers between devices with their start and end apart: 7, of which 0 were waited for; matrix products, arithmetic and copies ran while one was open for 17% of the time, Pallas kernels for 66%

profile of v2, /device:TPU:0, one launch (start us, length us, event | category | flops | bytes accessed | tf_op | source)
XLA Modules:
  0.0 162.1 jit_solution(1371575867994537961)
XLA Ops:
  0.6 0.7 fusion.47
  1.5 1.3 collective-permute-start.1
  2.9 3.0 %collective-permute-start = (bf16[8,128]{0,1:T(8,128)(2,1)S(1)}, bf16[8,128]{0,1:T(8,128)(2,1)S(1)}, u32[]{:S(2)}, u32[]{:S(2)}) collective-permute-start(bf16[8,128]{0,1:T(8,128)(2,1)S(1)} %copy.37), channel_id=1, source_target_pairs={{0,2},{2,4},{4,6},{1,3},{3,5},{5,7},{8,10},{10,12},{12,14},{9,11},... | collective-permute-start | bytes 6152 | tf_op jit(solution)/shard_map/ppermute | solution.py:21
  5.9 1.3 fusion.49
  9.2 0.9 copy.44
  10.1 1.5 fusion.27.x_ref
  11.7 14.1 %gather_framed.1 = bf16[8,64,640]{2,1,0:T(8,128)(2,1)} custom-call(bf16[64,384]{1,0:T(8,128)(2,1)} %fusion.27.x_ref), custom_call_target="tpu_custom_call" | custom-call | tf_op jit(solution)/shard_map/gather_framed/pallas_call | solution.py:165
  25.8 1.8 %constant_dynamic-slice_fusion.1 = (bf16[512,384]{1,0:T(8,128)(2,1)S(1)}, bf16[512,384]{1,0:T(8,128)(2,1)S(1)}, bf16[512,384]{1,0:T(8,128)(2,1)S(1)}) fusion(bf16[512,640]{1,0:T(8,128)(2,1)} %bitcast.82, s32[]{:T(128)S(6)} %select_n.64, s32[]{:T(128)S(6)} %select_n.65), kind=kLoop, calls=%fused_computation.76 | loop fusion | bytes 2359304 | tf_op jit(solution)/shard_map/dynamic_slice | solution.py:513
  28.0 0.8 copy-done.1
  28.9 3.1 %collective-permute-start.4 = (bf16[192,384]{1,0:T(8,128)(2,1)S(1)}, bf16[192,384]{1,0:T(8,128)(2,1)S(1)}, u32[]{:S(2)}, u32[]{:S(2)}) collective-permute-start(bf16[192,384]{1,0:T(8,128)(2,1)S(1)} %get-tuple-element.49), channel_id=1, source_target_pairs={{0,8},{8,16},{16,24},{24,0},{1,9},{9,17},{17,25},{25,1},{2,10},{10... | collective-permute-start | bytes 442376 | tf_op jit(solution)/shard_map/ppermute | solution.py:539
  32.0 1.1 collective-permute-start.5
  33.1 2.8 %collective-permute-start.6 = (bf16[192,384]{1,0:T(8,128)(2,1)S(1)}, bf16[192,384]{1,0:T(8,128)(2,1)S(1)}, u32[]{:S(2)}, u32[]{:S(2)}) collective-permute-start(bf16[192,384]{1,0:T(8,128)(2,1)S(1)} %get-tuple-element.48), channel_id=1, source_target_pairs={{0,24},{8,0},{16,8},{24,16},{1,25},{9,1},{17,9},{25,17},{2,26},{10... | collective-permute-start | bytes 442376 | tf_op jit(solution)/shard_map/ppermute | solution.py:539
  36.0 2.9 %select_reduce_fusion = s32[1536]{0:T(1024)S(1)} fusion(s32[1536]{0:T(1024)S(1)} %copy-done.8, s32[1536]{0:T(1024)S(1)} %copy-done.9), kind=kLoop, calls=%fused_computation | loop fusion | flops 14154240 | bytes 18432 | tf_op jit(solution)/shard_map/reduce_sum | solution.py:35
  39.5 0.8 convolution_bitcast_fusion.x_ref
  40.3 16.8 %embed.1 = f32[8,4,8,384]{3,2,1,0:T(8,128)} custom-call(f32[8,1,8,384]{3,2,1,0:T(8,128)} %convolution_bitcast_fusion.x_ref), custom_call_target="tpu_custom_call" | custom-call | tf_op jit(solution)/shard_map/embed/pallas_call | solution.py:290
  57.1 1.1 fusion.46
  58.3 0.7 pad_dynamic-slice_fusion.far_ref
  59.2 0.7 fusion.33.near_ref
  61.4 1.3 collective-permute-start.3
  62.7 4.5 %collective-permute-start.2 = (bf16[400,8]{0,1:T(8,128)(2,1)S(1)}, bf16[400,8]{0,1:T(8,128)(2,1)S(1)}, u32[]{:S(2)}, u32[]{:S(2)}) collective-permute-start(bf16[400,8]{0,1:T(8,128)(2,1)S(1)} %get-tuple-element.44), channel_id=1, source_target_pairs={{0,1},{1,8},{8,9},{9,16},{16,17},{17,24},{24,25},{2,3},{3,10},{10,... | collective-permute-start | bytes 19208 | tf_op jit(solution)/shard_map/ppermute | solution.py:21
  70.0 0.7 reshape.119.wfwd_ref
  70.8 0.7 reshape.120.wback_ref
  71.7 0.8 pad_convert_fusion.target_ref
  73.1 0.7 broadcast_in_dim.62.head_ref
  73.8 52.1 %band.1 = (f32[144,512]{1,0:T(8,128)}, f32[1,512]{1,0:T(1,128)}, f32[96,96]{1,0:T(8,128)}, f32[32,512]{1,0:T(8,128)}, f32[32,640]{1,0:T(8,128)}) custom-call(s32[1]{0:T(128)} %get-tuple-element.57.dil_ref, s32[2]{0:T(128)} %pad_add_fusion.place_ref, f32[1]{0:T(128)} %bitcast.1.denom_ref, f32[32,512]{1,0:T(8,128)} %fusion.33.near_ref, ...), custom_call_target="tpu_custom_call" | custom-call | flops 4000000000 | bytes 2000000 | tf_op jit(solution)/shard_map/band/pallas_call | solution.py:462
  125.9 1.0 slice.78
  127.0 1.0 dynamic_update_slice.19
  128.2 0.8 select_maximum_fusion.x_ref
  129.0 24.2 %grads.1 = f32[8,5,8,384]{3,2,1,0:T(8,128)} custom-call(f32[8,5,8,384]{3,2,1,0:T(8,128)} %select_maximum_fusion.x_ref), custom_call_target="tpu_custom_call" | custom-call | tf_op jit(solution)/shard_map/grads/pallas_call | solution.py:290
  153.3 1.0 slice.107
  154.7 0.9 slice.80
  156.1 0.8 copy.43
  (73 shorter events, 9.2 us)
Async XLA Ops:
  0.6 38.9 %copy-start = (bf16[2,64,32]{1,2,0:T(8,128)(2,1)S(1)}, bf16[2,64,32]{1,2,0:T(8,128)(2,1)}, u32[]{:S(2)}) copy-start(bf16[2,64,32]{1,2,0:T(8,128)(2,1)} %param.13) | copy-start | bytes 24580
  1.5 59.8 %collective-permute-start.1 = (bf16[8,128]{0,1:T(8,128)(2,1)S(1)}, bf16[8,128]{0,1:T(8,128)(2,1)S(1)}, u32[]{:S(2)}, u32[]{:S(2)}) collective-permute-start(bf16[8,128]{0,1:T(8,128)(2,1)S(1)} %copy.38), channel_id=1, source_target_pairs={{2,0},{4,2},{6,4},{3,1},{5,3},{7,5},{10,8},{12,10},{14,12},{11,9},... | collective-permute-start | bytes 6152 | tf_op jit(solution)/shard_map/ppermute | solution.py:23
  2.9 58.4 %collective-permute-start = (bf16[8,128]{0,1:T(8,128)(2,1)S(1)}, bf16[8,128]{0,1:T(8,128)(2,1)S(1)}, u32[]{:S(2)}, u32[]{:S(2)}) collective-permute-start(bf16[8,128]{0,1:T(8,128)(2,1)S(1)} %copy.37), channel_id=1, source_target_pairs={{0,2},{2,4},{4,6},{1,3},{3,5},{5,7},{8,10},{10,12},{12,14},{9,11},... | collective-permute-start | bytes 6152 | tf_op jit(solution)/shard_map/ppermute | solution.py:21
  25.8 1.8 %copy-start.6 = (bf16[64,384]{1,0:T(8,128)(2,1)S(1)}, bf16[64,384]{1,0:T(8,128)(2,1)}, u32[]{:S(2)}) copy-start(bf16[64,384]{1,0:T(8,128)(2,1)} %param.10) | copy-start | bytes 147460
  27.6 1.1 copy-start.1
  28.8 7.1 %copy-start.8 = (s32[1536]{0:T(1024)S(1)}, s32[1536]{0:T(1024)}, u32[]{:S(2)}) copy-start(s32[1536]{0:T(1024)} %param.17) | copy-start | bytes 18436
  28.8 7.1 %copy-start.9 = (s32[1536]{0:T(1024)S(1)}, s32[1536]{0:T(1024)}, u32[]{:S(2)}) copy-start(s32[1536]{0:T(1024)} %param.18) | copy-start | bytes 18436
  28.9 129.5 %collective-permute-start.4 = (bf16[192,384]{1,0:T(8,128)(2,1)S(1)}, bf16[192,384]{1,0:T(8,128)(2,1)S(1)}, u32[]{:S(2)}, u32[]{:S(2)}) collective-permute-start(bf16[192,384]{1,0:T(8,128)(2,1)S(1)} %get-tuple-element.49), channel_id=1, source_target_pairs={{0,8},{8,16},{16,24},{24,0},{1,9},{9,17},{17,25},{25,1},{2,10},{10... | collective-permute-start | bytes 442376 | tf_op jit(solution)/shard_map/ppermute | solution.py:539
  32.0 126.4 %collective-permute-start.5 = (bf16[192,384]{1,0:T(8,128)(2,1)S(1)}, bf16[192,384]{1,0:T(8,128)(2,1)S(1)}, u32[]{:S(2)}, u32[]{:S(2)}) collective-permute-start(bf16[192,384]{1,0:T(8,128)(2,1)S(1)} %get-tuple-element.50), channel_id=1, source_target_pairs={{0,16},{8,24},{16,0},{24,8},{1,17},{9,25},{17,1},{25,9},{2,18},{10... | collective-permute-start | bytes 442376 | tf_op jit(solution)/shard_map/ppermute | solution.py:539
  33.1 125.4 %collective-permute-start.6 = (bf16[192,384]{1,0:T(8,128)(2,1)S(1)}, bf16[192,384]{1,0:T(8,128)(2,1)S(1)}, u32[]{:S(2)}, u32[]{:S(2)}) collective-permute-start(bf16[192,384]{1,0:T(8,128)(2,1)S(1)} %get-tuple-element.48), channel_id=1, source_target_pairs={{0,24},{8,0},{16,8},{24,16},{1,25},{9,1},{17,9},{25,17},{2,26},{10... | collective-permute-start | bytes 442376 | tf_op jit(solution)/shard_map/ppermute | solution.py:539
  57.1 4.0 %copy-start.4 = (bf16[384,128]{1,0:T(8,128)(2,1)S(1)}, bf16[384,128]{1,0:T(8,128)(2,1)}, u32[]{:S(2)}) copy-start(bf16[384,128]{1,0:T(8,128)(2,1)} %param.16) | copy-start | bytes 294916
  58.2 9.7 %copy-start.2 = (bf16[9,32,32]{2,1,0:T(8,128)(2,1)S(1)}, bf16[9,32,32]{2,1,0:T(8,128)(2,1)}, u32[]{:S(2)}) copy-start(bf16[9,32,32]{2,1,0:T(8,128)(2,1)} %param.14) | copy-start | bytes 55300
  61.4 10.2 %collective-permute-start.3 = (bf16[400,8]{0,1:T(8,128)(2,1)S(1)}, bf16[400,8]{0,1:T(8,128)(2,1)S(1)}, u32[]{:S(2)}, u32[]{:S(2)}) collective-permute-start(bf16[400,8]{0,1:T(8,128)(2,1)S(1)} %get-tuple-element.45), channel_id=1, source_target_pairs={{1,0},{8,1},{9,8},{16,9},{17,16},{24,17},{25,24},{3,2},{10,3},{11,... | collective-permute-start | bytes 19208 | tf_op jit(solution)/shard_map/ppermute | solution.py:23
  62.7 8.9 %collective-permute-start.2 = (bf16[400,8]{0,1:T(8,128)(2,1)S(1)}, bf16[400,8]{0,1:T(8,128)(2,1)S(1)}, u32[]{:S(2)}, u32[]{:S(2)}) collective-permute-start(bf16[400,8]{0,1:T(8,128)(2,1)S(1)} %get-tuple-element.44), channel_id=1, source_target_pairs={{0,1},{1,8},{8,9},{9,16},{16,17},{17,24},{24,25},{2,3},{3,10},{10,... | collective-permute-start | bytes 19208 | tf_op jit(solution)/shard_map/ppermute | solution.py:21
  68.0 5.1 %copy-start.11 = (f32[32]{0:T(128)S(1)}, f32[32]{0:T(128)}, u32[]{:S(2)}) copy-start(f32[32]{0:T(128)} %param.15) | copy-start | bytes 388
  125.9 1.1 copy-start.7
  126.9 1.2 copy-start.5
  126.9 1.2 copy-start.10
  129.0 25.5 %copy-start.3 = (f32[144,512]{1,0:T(8,128)S(1)}, f32[144,512]{1,0:T(8,128)}, u32[]{:S(2)}) copy-start(f32[144,512]{1,0:T(8,128)} %get-tuple-element.10) | copy-start | bytes 884740

commit v3 on v2

--- a/solution.py
+++ b/solution.py
@@ -310,179 +310,252 @@
     return (value + step - 1) // step * step
 
 
+RING = 32
+UNROLL = 4
+
+
 def band_body(
     edge,
     rows,
-    unroll,
     dil_ref,
     place_ref,
     denom_ref,
-    near_ref,
-    far_ref,
-    fmask_ref,
-    lanes_ref,
-    limit_ref,
+    embed_ref,
+    bins_ref,
     target_ref,
     head_ref,
-    wfwd_ref,
-    wback_ref,
+    taps_ref,
     pred_ref,
     err_ref,
     gband_ref,
     gnear_ref,
     gfar_ref,
+    near_ext,
+    far_ext,
     far_rolled,
     mask_rolled,
     near_shift,
+    near_own,
     stack,
-    resid_acc,
-    dact_acc,
+    sums,
+    backs,
     own_grad,
+    block,
 ):
-    chans, width = near_ref.shape
-    wide = far_ref.shape[1]
+    group, encs, rows_piece, span = embed_ref.shape
+    chans = head_ref.shape[0]
+    width = gnear_ref.shape[1]
+    wide = gfar_ref.shape[1]
+    lag = edge + UNROLL
     d = dil_ref[0]
-    offs_first = place_ref[0]
-    offs_count = place_ref[1]
+    row_start = pl.multiple_of(place_ref[0], 128)
+    offs_first = place_ref[1]
+    offs_count = place_ref[2]
+    far_start = pl.multiple_of(row_start + offs_first, 128)
     denom = denom_ref[0]
-    all_rows = rows + 4 * edge
-    last = rows + 3 * edge
-
-    def loop(start, stop, body, init):
-        def step(index, carry):
-            for inner in range(unroll):
-                carry = body(start + index * unroll + inner, carry)
-            return carry
-
-        return lax.fori_loop(0, (stop - start) // unroll, step, init)
-
-    near_shift[1] = near_ref[...]
-    near_shift[0] = pltpu.roll(near_ref[...], d, 1)
-    near_shift[2] = pltpu.roll(near_ref[...], width - d, 1)
-
-    def fill(k, carry):
-        shift = lax.rem(wide - k, wide)
-        far_rolled[k] = pltpu.roll(far_ref[...], shift, 1)[:, :width].astype(jnp.bfloat16)
-        mask_rolled[k] = pltpu.roll(fmask_ref[...], shift, 1)[:, :width]
+    seq = encs * span
+
+    near_ext[...] = jnp.zeros(near_ext.shape, jnp.float32)
+    far_ext[...] = jnp.zeros(far_ext.shape, jnp.float32)
+    for g in range(group):
+        first = g * rows_piece
+        for z in range(encs):
+            here = slice(128 + z * span, 128 + (z + 1) * span)
+            if first < chans:
+                near_ext[first : first + rows_piece, here] = embed_ref[g, z]
+            else:
+                far_ext[first - chans : first - chans + rows_piece, here] = embed_ref[g, z]
+    near_ext[chans : chans + 8, 128 : 128 + seq] = bins_ref[...].astype(jnp.float32)
+    far_ext[chans : chans + 8, 128 : 128 + seq] = bins_ref[...].astype(jnp.float32)
+    around = near_ext[:, pl.ds(row_start, width + 128)]
+    around = pltpu.roll(around, width + 2 * edge, 1)[:, :width]
+    ahead = far_ext[:, pl.ds(far_start, wide + 128)]
+    ahead = pltpu.roll(ahead, wide + 5 * edge, 1)[:, :wide]
+    spots = lax.broadcasted_iota(jnp.int32, (1, width), 1)
+    bin_ids = row_start - 2 * edge + spots
+    near = jnp.where((bin_ids >= 0) & (bin_ids < seq), around[:chans], -jnp.inf)
+    own_lane = (spots >= 2 * edge) & (spots < width - 128 + 2 * edge)
+    framed_lane = (spots >= edge) & (spots < width - 128 + 3 * edge)
+    scored = jnp.where(framed_lane, around[chans : chans + 1], 0.0)
+    limit = around[chans + 1 : chans + 2]
+    near_own[0] = near
+    near_own[1] = jnp.where(own_lane, near, -jnp.inf)
+    near_shift[1] = near.astype(jnp.bfloat16)
+    near_shift[0] = pltpu.roll(near, d, 1).astype(jnp.bfloat16)
+    near_shift[2] = pltpu.roll(near, width - d, 1).astype(jnp.bfloat16)
+    far_ext[:, :wide] = ahead
+
+    block[...] = jnp.zeros(block.shape, jnp.float32)
+    for a in range(3):
+        for b in range(3):
+            tap = taps_ref[3 * a + b].astype(jnp.float32)
+            block[0, a * chans : (a + 1) * chans, b * chans : (b + 1) * chans] = tap
+            block[1, b * chans : (b + 1) * chans, a * chans : (a + 1) * chans] = tap
+    forward_taps = block[0].T[: 3 * chans, : 3 * chans].astype(jnp.bfloat16)
+    back_taps = block[1][: 3 * chans, : 3 * chans].astype(jnp.bfloat16)
+
+    def fill(index, carry):
+        for u in range(UNROLL):
+            k = index * UNROLL + u
+            turned = pltpu.roll(far_ext[:, :wide], lax.rem(wide - k, wide), 1)[:, :width]
+            far_rolled[k] = turned[:chans].astype(jnp.bfloat16)
+            mask_rolled[k] = turned[chans : chans + 8]
         return carry
 
-    loop(0, all_rows + 2 * edge, fill, 0)
-
-    def clear(r, carry):
-        resid_acc[r + edge] = near_ref[...] + far_rolled[r + edge].astype(jnp.float32)
-        dact_acc[r] = jnp.zeros((chans, width), jnp.float32)
-        return carry
-
-    loop(0, all_rows, clear, 0)
-    for r in list(range(edge)) + list(range(last, all_rows)):
-        own_grad[r] = jnp.zeros((chans, width), jnp.bfloat16)
-
-    def forward(r, carry):
-        offs = offs_first + r - 2 * edge
-        inside = jnp.where((offs >= 0) & (offs < offs_count), 1.0, 0.0)
-        for a in range(3):
-            cells = near_shift[a] + far_rolled[r + edge + (a - 1) * d].astype(jnp.float32)
-            cells = jnp.maximum(cells, 0.0) * inside
-            stack[r, a * chans : (a + 1) * chans, :] = cells.astype(jnp.bfloat16)
-        taps = jnp.dot(wfwd_ref[...], stack[r], preferred_element_type=jnp.float32)
-        for b in range(3):
-            spot = r + edge - (b - 1) * d
-            resid_acc[spot] = resid_acc[spot] + taps[b * chans : (b + 1) * chans]
-        return carry
-
-    loop(0, all_rows, forward, 0)
-
-    def middle(r, err):
-        resid = resid_acc[r + edge]
-        head = head_ref[...]
-        pred = jnp.sum(head * jnp.maximum(resid, 0.0), axis=0, keepdims=True)
-        pred_ref[pl.ds(r - edge, 1), :] = pred
-        offs = offs_first + r - 2 * edge
-        inside = jnp.where((offs >= 0) & (offs < offs_count), 1.0, 0.0)
-        own_row = jnp.where((r >= 2 * edge) & (r < rows + 2 * edge), 1.0, 0.0)
-        weight = (
-            lanes_ref[0:1, :]
-            * mask_rolled[r + edge][0:1, :]
-            * jnp.where(offs < limit_ref[...], inside, 0.0)
-        )
-        differ = pred - target_ref[pl.ds(r - edge, 1), :]
-        own = lanes_ref[1:2, :] * own_row
-        err = err + weight * differ * differ * own
-        dpred = 2.0 * weight * differ / denom
-        dres = jnp.where(resid > 0.0, head * dpred, 0.0).astype(jnp.bfloat16).astype(jnp.float32)
-        own_grad[r] = (dres * own).astype(jnp.bfloat16)
-        shifted = jnp.concatenate(
-            [
-                pltpu.roll(dres, width - d, 1).astype(jnp.bfloat16),
-                dres.astype(jnp.bfloat16),
-                pltpu.roll(dres, d, 1).astype(jnp.bfloat16),
-            ],
-            axis=0,
-        )
-        taps = jnp.dot(wback_ref[...], shifted, preferred_element_type=jnp.float32)
-        for b in range(3):
-            spot = r + (b - 1) * d
-            dact_acc[spot] = dact_acc[spot] + taps[b * chans : (b + 1) * chans]
-        return err
-
-    err = loop(edge, last, middle, jnp.zeros((1, width), jnp.float32))
-    err_ref[...] = err
-
-    def weigh(r, total):
-        grads = jnp.concatenate([own_grad[r - (b - 1) * d] for b in range(3)], axis=0)
-        return total + lax.dot_general(
-            stack[r], grads, (((1,), (1,)), ((), ())), preferred_element_type=jnp.float32
-        )
-
-    gband_ref[...] = loop(edge, last, weigh, jnp.zeros((3 * chans, 3 * chans), jnp.float32))
-
-    own_near = jnp.where(lanes_ref[1:2, :] > 0.0, near_ref[...], -jnp.inf)
+    total = rows + 6 * edge
+    lax.fori_loop(0, (total + 2 * edge) // UNROLL, fill, 0)
+    stack[...] = jnp.zeros(stack.shape, jnp.bfloat16)
+    own_grad[...] = jnp.zeros(own_grad.shape, jnp.bfloat16)
+    gband_ref[...] = jnp.zeros(gband_ref.shape, jnp.float32)
     gnear_ref[...] = jnp.zeros(gnear_ref.shape, jnp.float32)
     gfar_ref[...] = jnp.zeros(gfar_ref.shape, jnp.float32)
+    head = head_ref[...]
     blank = jnp.zeros((chans, wide - width), jnp.float32)
-    near_shift[0] = own_near
-
-    def collect(r, carry):
-        pair = near_shift[0] + far_rolled[r + edge].astype(jnp.float32)
-        dpair = own_grad[r].astype(jnp.float32) + jnp.where(pair > 0.0, dact_acc[r], 0.0)
-        gnear_ref[...] += dpair
-        gfar_ref[...] += pltpu.roll(jnp.concatenate([dpair, blank], axis=1), r + edge, 1)
-        return carry
-
-    loop(2 * edge, rows + 2 * edge, collect, 0)
-
-
-def band(near, far, fmask, lanes, limits, target, head, wfwd, wback, dil, place, denom, rows):
-    chans, width = near.shape
-    wide = far.shape[1]
+
+    def slot(r):
+        return lax.rem(r + 2 * RING, RING)
+
+    def owned(r):
+        return (r >= 2 * edge) & (r < rows + 2 * edge)
+
+    def step(index, err):
+        start = index * UNROLL
+        near_sum = jnp.zeros((chans, width), jnp.float32)
+        far_sum = jnp.zeros((chans, wide), jnp.float32)
+        cells_old = []
+        grads_old = []
+        for u in range(UNROLL):
+            r = start + u - 2 * lag
+            pair = near_own[1] + far_rolled[jnp.maximum(r + edge, 0)].astype(jnp.float32)
+            dact = (
+                backs[slot(r + d), :chans]
+                + backs[slot(r), chans : 2 * chans]
+                + backs[slot(r - d), 2 * chans :]
+            )
+            dpair = own_grad[slot(r)].astype(jnp.float32) + jnp.where(pair > 0.0, dact, 0.0)
+            dpair = jnp.where(owned(r), dpair, 0.0)
+            near_sum = near_sum + dpair
+            far_sum = far_sum + pltpu.roll(
+                jnp.concatenate([dpair, blank], axis=1), lax.rem(r + edge + wide, wide), 1
+            )
+            cells_old.append(stack[slot(r)])
+            grads_old.append(
+                jnp.concatenate(
+                    [own_grad[slot(r + d)], own_grad[slot(r)], own_grad[slot(r - d)]], axis=0
+                )
+            )
+        gnear_ref[...] += near_sum
+        gfar_ref[...] += far_sum
+        gband_ref[...] += lax.dot_general(
+            jnp.concatenate(cells_old, axis=1),
+            jnp.concatenate(grads_old, axis=1),
+            (((1,), (1,)), ((), ())),
+            preferred_element_type=jnp.float32,
+        )
+
+        shifted = []
+        for u in range(UNROLL):
+            r = start + u - lag
+            spot = jnp.maximum(r + edge, 0)
+            resid = near_own[0] + far_rolled[spot].astype(jnp.float32)
+            resid = resid + (
+                sums[slot(r - d), :chans]
+                + sums[slot(r), chans : 2 * chans]
+                + sums[slot(r + d), 2 * chans :]
+            )
+            pred = jnp.sum(head * jnp.maximum(resid, 0.0), axis=0, keepdims=True)
+            pred_ref[pl.ds(start + u, 1), :] = pred
+            offs = offs_first + r - 2 * edge
+            inside = jnp.where((offs >= 0) & (offs < offs_count), 1.0, 0.0)
+            weight = (
+                scored
+                * mask_rolled[spot][0:1, :]
+                * jnp.where(offs.astype(jnp.float32) < limit, inside, 0.0)
+            )
+            differ = pred - target_ref[pl.ds(start + u, 1), :]
+            own = own_lane & owned(r)
+            err = err + jnp.where(own, weight * differ * differ, 0.0)
+            dpred = 2.0 * weight * differ / denom
+            dres = jnp.where(resid > 0.0, head * dpred, 0.0)
+            dres = dres.astype(jnp.bfloat16).astype(jnp.float32)
+            own_grad[slot(r)] = jnp.where(own, dres, 0.0).astype(jnp.bfloat16)
+            shifted.append(
+                jnp.concatenate(
+                    [
+                        pltpu.roll(dres, width - d, 1).astype(jnp.bfloat16),
+                        dres.astype(jnp.bfloat16),
+                        pltpu.roll(dres, d, 1).astype(jnp.bfloat16),
+                    ],
+                    axis=0,
+                )
+            )
+        backed = jnp.dot(
+            back_taps, jnp.concatenate(shifted, axis=1), preferred_element_type=jnp.float32
+        )
+
+        fresh = []
+        for u in range(UNROLL):
+            r = start + u
+            offs = offs_first + r - 2 * edge
+            inside = jnp.where((offs >= 0) & (offs < offs_count), 1.0, 0.0)
+            keep = jnp.full((chans, width), inside, jnp.float32).astype(jnp.bfloat16)
+            parts = []
+            for a in range(3):
+                cells = near_shift[a] + far_rolled[r + edge + (a - 1) * d]
+                parts.append(jnp.maximum(cells, 0.0) * keep)
+            fresh.append(jnp.concatenate(parts, axis=0))
+        summed = jnp.dot(
+            forward_taps, jnp.concatenate(fresh, axis=1), preferred_element_type=jnp.float32
+        )
+        for u in range(UNROLL):
+            lanes = slice(u * width, (u + 1) * width)
+            backs[slot(start + u - lag)] = backed[:, lanes]
+            sums[slot(start + u)] = summed[:, lanes]
+            stack[slot(start + u)] = fresh[u]
+        return err
+
+    err_ref[...] = lax.fori_loop(
+        0, total // UNROLL, step, jnp.zeros((1, width), jnp.float32)
+    )
+
+
+def band(pieces, bins, target, head, conv_two, dil, place, denom, rows, tile_rows, extent):
+    chans = head.shape[0]
     edge = LARGEST_DILATION
-    all_rows = rows + 4 * edge
+    width = tile_rows + 128
+    wide = round_up(tile_rows + rows + 10 * edge, 128)
+    total = rows + 6 * edge
+    ext = bins.shape[1] + extent + wide + 128
     smem = pl.BlockSpec(memory_space=pltpu.SMEM)
     vmem = pl.BlockSpec(memory_space=pltpu.VMEM)
     return pl.pallas_call(
-        functools.partial(band_body, edge, rows, 4),
+        functools.partial(band_body, edge, rows),
         out_shape=(
-            jax.ShapeDtypeStruct((rows + 2 * edge, width), jnp.float32),
+            jax.ShapeDtypeStruct((total, width), jnp.float32),
             jax.ShapeDtypeStruct((1, width), jnp.float32),
             jax.ShapeDtypeStruct((3 * chans, 3 * chans), jnp.float32),
             jax.ShapeDtypeStruct((chans, width), jnp.float32),
             jax.ShapeDtypeStruct((chans, wide), jnp.float32),
         ),
-        in_specs=[smem] * 3 + [vmem] * 9,
+        in_specs=[smem] * 3 + [vmem] * 5,
         out_specs=(vmem,) * 5,
         scratch_shapes=[
-            pltpu.VMEM((all_rows + 2 * edge, chans, width), jnp.bfloat16),
-            pltpu.VMEM((all_rows + 2 * edge, 8, width), jnp.float32),
-            pltpu.VMEM((3, chans, width), jnp.float32),
-            pltpu.VMEM((all_rows, 3 * chans, width), jnp.bfloat16),
-            pltpu.VMEM((all_rows + 2 * edge, chans, width), jnp.float32),
-            pltpu.VMEM((all_rows, chans, width), jnp.float32),
-            pltpu.VMEM((all_rows, chans, width), jnp.bfloat16),
+            pltpu.VMEM((chans + 8, ext), jnp.float32),
+            pltpu.VMEM((chans + 8, ext), jnp.float32),
+            pltpu.VMEM((total + 2 * edge, chans, width), jnp.bfloat16),
+            pltpu.VMEM((total + 2 * edge, 8, width), jnp.float32),
+            pltpu.VMEM((3, chans, width), jnp.bfloat16),
+            pltpu.VMEM((2, chans, width), jnp.float32),
+            pltpu.VMEM((RING, 3 * chans, width), jnp.bfloat16),
+            pltpu.VMEM((RING, 3 * chans, width), jnp.float32),
+            pltpu.VMEM((RING, 3 * chans, width), jnp.float32),
+            pltpu.VMEM((RING, chans, width), jnp.bfloat16),
+            pltpu.VMEM((2, 128, 128), jnp.float32),
         ],
-        compiler_params=pltpu.CompilerParams(vmem_limit_bytes=60 * 1024 * 1024),
+        compiler_params=pltpu.CompilerParams(vmem_limit_bytes=56 * 1024 * 1024),
         cost_estimate=pl.CostEstimate(flops=4000000000, bytes_accessed=2000000, transcendentals=0),
         name="band",
-    )(dil, place, denom, near, far, fmask, lanes, limits, target, head, wfwd, wback)
+    )(dil, place, denom, pieces, bins, target, head, conv_two)
 
 
 def shards(
@@ -523,13 +596,13 @@
     pieces = exchange(
         partial_embed.reshape(group, 1, rows_piece, encoder_bins), encs, bins, offs, False, 1, "embed"
     )
-    embed = jnp.transpose(pieces, (0, 2, 1, 3)).reshape(2 * second_channels, encs * encoder_bins)
+    framed, hidden_sent, pieces = lax.optimization_barrier((framed, hidden, pieces))
     enc_index = lax.axis_index("enc")
     share = width_in // encs
 
     def parcel(owner):
         rows = lax.dynamic_slice(framed, (owner * share, 128), (share, encoder_bins))
-        return jnp.concatenate([rows, hidden], axis=0)
+        return jnp.concatenate([rows, hidden_sent], axis=0)
 
     whole_side = jnp.zeros((share + chans, encs * encoder_bins), jnp.bfloat16)
     whole_side = lax.dynamic_update_slice(
@@ -543,67 +616,37 @@
         )
         origin = lax.rem(enc_index + encs - hop, encs)
         whole_side = lax.dynamic_update_slice(whole_side, arrived, (0, origin * encoder_bins))
-    sequence_length = embed.shape[1]
+    sequence_length = encs * encoder_bins
     window_extent = tile_cols * encs * offs
     row_start = lax.axis_index("bin") * tile_rows
     offs_start = (lax.axis_index("enc") * lax.axis_size("off") + lax.axis_index("off")) * tile_cols
     edge = LARGEST_DILATION
-    width = round_up(tile_rows + 4 * edge, 128)
-    wide = round_up(tile_rows + tile_cols + 10 * edge, 128)
-    bin_ids = row_start - 2 * edge + jnp.arange(width, dtype=jnp.int32)
-    inside = (bin_ids >= 0) & (bin_ids < sequence_length)
-    near = lax.dynamic_slice_in_dim(
-        jnp.pad(embed[:second_channels], ((0, 0), (2 * edge, width))),
-        row_start,
-        width,
-        1,
-    )
-    near = jnp.where(inside[None, :], near, -jnp.inf)
-    far = lax.dynamic_slice_in_dim(
-        jnp.pad(
-            embed[second_channels:], ((0, 0), (5 * edge, window_extent + wide))
-        ),
-        row_start + offs_start,
-        wide,
-        1,
-    )
-    mask_float = valid_bins.astype(jnp.float32)
-    far_mask = lax.dynamic_slice_in_dim(
-        jnp.pad(mask_float, (5 * edge, window_extent + wide)), row_start + offs_start, wide
-    )
-    near_mask = lax.dynamic_slice_in_dim(
-        jnp.pad(mask_float, (2 * edge, width)), row_start, width
-    )
-    limits = lax.dynamic_slice_in_dim(jnp.pad(offset_limit, (2 * edge, width)), row_start, width)
-    spots = jnp.arange(width, dtype=jnp.int32)
-    framed_lane = (spots >= edge) & (spots < tile_rows + 3 * edge)
-    own_lane = (spots >= 2 * edge) & (spots < tile_rows + 2 * edge)
-    lanes = jnp.stack([jnp.where(framed_lane, near_mask, 0.0), own_lane.astype(jnp.float32)])
-    lanes = jnp.pad(lanes, ((0, 6), (0, 0)))
+    width = tile_rows + 128
+    bin_rows = jnp.pad(jnp.stack([valid_bins, offset_limit]), ((0, 6), (0, 0)))
     denom = 1.0 + count_cells(valid_bins, offset_limit)
     framed_target = with_halo(target, (("bin", 0), (("enc", "off"), 1)), edge)
+    first_row = 2 * edge + UNROLL
     target_rows = jnp.pad(
-        framed_target.T.astype(jnp.float32), ((0, 0), (edge, width - tile_rows - 3 * edge))
-    )
-    taps = conv_two.reshape(3, 3, second_channels, second_channels)
-    weight_fwd = jnp.transpose(taps, (1, 3, 0, 2)).reshape(3 * second_channels, 3 * second_channels)
-    weight_back = jnp.transpose(taps, (1, 2, 0, 3)).reshape(3 * second_channels, 3 * second_channels)
+        framed_target.T.astype(jnp.float32),
+        ((first_row, 2 * edge - UNROLL), (edge, width - tile_rows - 3 * edge)),
+    )
     pred_rows, error_lanes, grad_taps, near_lanes, far_lanes = band(
-        near,
-        far,
-        jnp.broadcast_to(far_mask[None, :], (8, wide)),
-        lanes,
-        limits[None, :],
+        pieces,
+        bin_rows,
         target_rows,
-        jnp.broadcast_to(head_weight[:, None], (second_channels, width)),
-        weight_fwd,
-        weight_back,
+        head_weight.reshape(second_channels, 1),
+        conv_two,
         second_dilation.reshape(1),
-        jnp.stack([offs_start, jnp.full((), window_extent, jnp.int32)]).astype(jnp.int32),
+        jnp.stack([row_start, offs_start, jnp.full((), window_extent, jnp.int32)]).astype(jnp.int32),
         denom.reshape(1),
         tile_cols,
-    )
-    prediction = pred_rows[edge : edge + tile_cols, 2 * edge : 2 * edge + tile_rows].T
+        tile_rows,
+        window_extent,
+    )
+    first_own = first_row + edge
+    prediction = pred_rows[
+        first_own : first_own + tile_cols, 2 * edge : 2 * edge + tile_rows
+    ].T
     near_grad = near_lanes[:, 2 * edge : 2 * edge + tile_rows]
     far_grad = far_lanes[:, 5 * edge : 5 * edge + tile_rows + tile_cols - 1]
     buffer = jnp.zeros((2 * second_channels, sequence_length + window_extent), jnp.float32)

time: 163 us -> 147 us (0.902)
  local copies, waits for them, and re-layouts: 17.4 us -> 11.8 us
  Pallas kernels: 107 us -> 102 us
  starting transfers between devices: 17.2 us -> 14.1 us
    pallas_call x1, Pallas kernels: 52.1 us -> 44.8 us  [band(): pl.pallas_call(functools.partial(band_body, edge, rows), out_shape=(jax.S...]
    ppermute x3, starting transfers between devices: 7.04 us -> 4.01 us  [shards(): lax.ppermute(parcel(lax.rem(enc_index + hop, encs)), 'enc', [(i, (i + hop...]
    pallas_call x2, Pallas kernels: 41 us -> 42.9 us  [exchange(): pl.pallas_call(functools.partial(exchange_body, encs, bins, offs, spread)...]
  transfers between devices with their start and end apart: 7 -> 7, of which waited for: 0 -> 0; matrix products, arithmetic and copies ran while one was open for 17% -> 14% of each run, Pallas kernels for 66% -> 69%
where the time goes in v3:
time: 147 us
  Pallas kernels  102 us (69%)
  starting transfers between devices  14.1 us (10%)
  local copies, waits for them, and re-layouts  11.8 us (8%)
  other arithmetic  9.59 us (7%)
  between operations  6.81 us (5%)
  matrix products  2.48 us (2%)
    pallas_call x1, Pallas kernels, band(): pl.pallas_call(functools.partial(band_body, edge, rows), out_shape=(jax.S...  44.8 us
    pallas_call x2, Pallas kernels, exchange(): pl.pallas_call(functools.partial(exchange_body, encs, bins, offs, spread)...  42.9 us
    pallas_call x1, Pallas kernels, gather_framed(): pl.pallas_call(functools.partial(gather_body, encs, bins, offs), out_shap...  14.1 us
    ppermute x2, starting transfers between devices, with_halo(): lax.ppermute(tail, axis, [(i, (i + 1) % count) for i in range(ends)])  7.57 us
    ppermute x3, starting transfers between devices, shards(): lax.ppermute(parcel(lax.rem(enc_index + hop, encs)), 'enc', [(i, (i + hop...  4.01 us
  transfers between devices with their start and end apart: 7, of which 0 were waited for; matrix products, arithmetic and copies ran while one was open for 14% of the time, Pallas kernels for 69%

profile of v3, /device:TPU:0, one launch (start us, length us, event | category | flops | bytes accessed | tf_op | source)
XLA Modules:
  0.0 146.6 jit_solution(14383175618521145096)
XLA Ops:
  0.7 0.7 fusion.40
  1.5 1.3 collective-permute-start.1
  2.9 3.0 %collective-permute-start = (bf16[8,128]{0,1:T(8,128)(2,1)S(1)}, bf16[8,128]{0,1:T(8,128)(2,1)S(1)}, u32[]{:S(2)}, u32[]{:S(2)}) collective-permute-start(bf16[8,128]{0,1:T(8,128)(2,1)S(1)} %copy.34), channel_id=1, source_target_pairs={{0,2},{2,4},{4,6},{1,3},{3,5},{5,7},{8,10},{10,12},{12,14},{9,11},... | collective-permute-start | bytes 6152 | tf_op jit(solution)/shard_map/ppermute | solution.py:21
  6.0 1.4 fusion.41
  9.3 1.5 %fusion.27.x_ref = bf16[64,384]{1,0:T(8,128)(2,1)} fusion(bf16[64,384]{1,0:T(8,128)(2,1)} %param.10, f32[64]{0:T(128)} %param.11), kind=kLoop, calls=%fused_computation.40 | loop fusion | flops 270336 | bytes 98560 | tf_op jit(solution)/shard_map/convert_element_type | solution.py:579
  10.9 14.1 %gather_framed.1 = bf16[8,64,640]{2,1,0:T(8,128)(2,1)} custom-call(bf16[64,384]{1,0:T(8,128)(2,1)} %fusion.27.x_ref), custom_call_target="tpu_custom_call" | custom-call | tf_op jit(solution)/shard_map/gather_framed/pallas_call | solution.py:165
  25.1 1.8 %constant_dynamic-slice_fusion.1 = (bf16[512,384]{1,0:T(8,128)(2,1)S(1)}, bf16[512,384]{1,0:T(8,128)(2,1)S(1)}, bf16[512,384]{1,0:T(8,128)(2,1)S(1)}) fusion(bf16[512,640]{1,0:T(8,128)(2,1)} %bitcast.74, s32[]{:T(128)S(6)} %select_n.47, s32[]{:T(128)S(6)} %select_n.48), kind=kLoop, calls=%fused_computation.65 | loop fusion | bytes 2359304 | tf_op jit(solution)/shard_map/dynamic_slice | solution.py:586
  27.2 0.8 convolution_bitcast_fusion.x_ref
  28.0 18.9 %embed.1.embed_ref = f32[8,4,8,384]{3,2,1,0:T(8,128)} custom-call(f32[8,1,8,384]{3,2,1,0:T(8,128)} %convolution_bitcast_fusion.x_ref), custom_call_target="tpu_custom_call" | custom-call | tf_op jit(solution)/shard_map/embed/pallas_call | solution.py:290
  47.5 2.4 %collective-permute-start.5 = (bf16[192,384]{1,0:T(8,128)(2,1)S(1)}, bf16[192,384]{1,0:T(8,128)(2,1)S(1)}, u32[]{:S(2)}, u32[]{:S(2)}) collective-permute-start(bf16[192,384]{1,0:T(8,128)(2,1)S(1)} %get-tuple-element.54), channel_id=1, source_target_pairs={{0,16},{8,24},{16,0},{24,8},{1,17},{9,25},{17,1},{25,9},{2,18},{10... | collective-permute-start | bytes 442376 | tf_op jit(solution)/shard_map/ppermute | solution.py:612
  49.8 1.3 collective-permute-start.6
  51.2 2.9 %select_reduce_fusion = s32[1536]{0:T(1024)S(1)} fusion(s32[1536]{0:T(1024)S(1)} %copy-done.8, s32[1536]{0:T(1024)S(1)} %copy-done.9), kind=kLoop, calls=%fused_computation | loop fusion | flops 14154240 | bytes 18432 | tf_op jit(solution)/shard_map/reduce_sum | solution.py:35
  54.1 0.6 multiply_reduce_fusion
  55.0 1.3 collective-permute-start.3
  56.3 4.5 %collective-permute-start.2 = (bf16[400,8]{0,1:T(8,128)(2,1)S(1)}, bf16[400,8]{0,1:T(8,128)(2,1)S(1)}, u32[]{:S(2)}, u32[]{:S(2)}) collective-permute-start(bf16[400,8]{0,1:T(8,128)(2,1)S(1)} %get-tuple-element.48), channel_id=1, source_target_pairs={{0,1},{1,8},{8,9},{9,16},{16,17},{17,24},{24,25},{2,3},{3,10},{10,... | collective-permute-start | bytes 19208 | tf_op jit(solution)/shard_map/ppermute | solution.py:21
  60.8 0.6 pad_add_fusion.1.place_ref
  63.4 0.6 pad.22.bins_ref
  64.0 0.7 copy.37.head_ref
  64.9 0.9 pad_convert_fusion.target_ref
  65.8 44.8 %band.1 = (f32[176,512]{1,0:T(8,128)}, f32[1,512]{1,0:T(1,128)}, f32[96,96]{1,0:T(8,128)}, f32[32,512]{1,0:T(8,128)}, f32[32,640]{1,0:T(8,128)}) custom-call(s32[1]{0:T(128)} %get-tuple-element.59.dil_ref, s32[3]{0:T(128)} %pad_add_fusion.1.place_ref, f32[1]{0:T(128)} %bitcast.2.denom_ref, f32[8,4,8,384]{3,2,1,0:T(8,128)} %embed.1.embed_ref, ...), custom_call_target="tpu_custom_call" | custom-call | flops 4000000000 | bytes 2000000 | tf_op jit(solution)/shard_map/band/pallas_call | solution.py:531
  110.5 1.0 slice.62
  111.7 1.0 dynamic_update_slice.19
  112.9 0.8 select_maximum_fusion.x_ref
  113.7 24.0 %grads.1 = f32[8,5,8,384]{3,2,1,0:T(8,128)} custom-call(f32[8,5,8,384]{3,2,1,0:T(8,128)} %select_maximum_fusion.x_ref), custom_call_target="tpu_custom_call" | custom-call | tf_op jit(solution)/shard_map/grads/pallas_call | solution.py:290
  137.7 1.0 slice.89
  139.1 0.8 slice.64
  139.9 0.6 slice_reduce_fusion
  140.5 0.8 copy.39
  142.1 0.7 copy.38
  143.4 0.4 convolution_bitcast_fusion.1
  144.2 0.6 pad_maximum_fusion.5
  144.8 0.6 pad_maximum_fusion.4
  (63 shorter events, 3.2 us)
Async XLA Ops:
  0.6 26.5 %copy-start = (bf16[2,64,32]{1,2,0:T(8,128)(2,1)S(1)}, bf16[2,64,32]{1,2,0:T(8,128)(2,1)}, u32[]{:S(2)}) copy-start(bf16[2,64,32]{1,2,0:T(8,128)(2,1)} %param.13) | copy-start | bytes 24580
  0.6 24.3 %copy-start.2 = (bf16[3,64,512]{2,1,0:T(8,128)(2,1)S(1)}, bf16[3,64,512]{2,1,0:T(8,128)(2,1)}, u32[]{:S(2)}) copy-start(bf16[3,64,512]{2,1,0:T(8,128)(2,1)} %param.12) | copy-start | bytes 589828
  1.5 53.4 %collective-permute-start.1 = (bf16[8,128]{0,1:T(8,128)(2,1)S(1)}, bf16[8,128]{0,1:T(8,128)(2,1)S(1)}, u32[]{:S(2)}, u32[]{:S(2)}) collective-permute-start(bf16[8,128]{0,1:T(8,128)(2,1)S(1)} %copy.35), channel_id=1, source_target_pairs={{2,0},{4,2},{6,4},{3,1},{5,3},{7,5},{10,8},{12,10},{14,12},{11,9},... | collective-permute-start | bytes 6152 | tf_op jit(solution)/shard_map/ppermute | solution.py:23
  2.9 52.0 %collective-permute-start = (bf16[8,128]{0,1:T(8,128)(2,1)S(1)}, bf16[8,128]{0,1:T(8,128)(2,1)S(1)}, u32[]{:S(2)}, u32[]{:S(2)}) collective-permute-start(bf16[8,128]{0,1:T(8,128)(2,1)S(1)} %copy.34), channel_id=1, source_target_pairs={{0,2},{2,4},{4,6},{1,3},{3,5},{5,7},{8,10},{10,12},{12,14},{9,11},... | collective-permute-start | bytes 6152 | tf_op jit(solution)/shard_map/ppermute | solution.py:21
  25.0 1.8 %copy-start.6 = (bf16[64,384]{1,0:T(8,128)(2,1)S(1)}, bf16[64,384]{1,0:T(8,128)(2,1)}, u32[]{:S(2)}) copy-start(bf16[64,384]{1,0:T(8,128)(2,1)} %param.10) | copy-start | bytes 147460
  27.2 19.7 %copy-start.1 = (bf16[8,64,640]{2,1,0:T(8,128)(2,1)S(1)}, bf16[8,64,640]{2,1,0:T(8,128)(2,1)}, u32[]{:S(2)}) copy-start(bf16[8,64,640]{2,1,0:T(8,128)(2,1)} %gather_framed.1) | copy-start | bytes 1966084
  47.0 4.1 %copy-start.9 = (s32[1536]{0:T(1024)S(1)}, s32[1536]{0:T(1024)}, u32[]{:S(2)}) copy-start(s32[1536]{0:T(1024)} %param.18) | copy-start | bytes 18436
  47.0 4.1 %copy-start.8 = (s32[1536]{0:T(1024)S(1)}, s32[1536]{0:T(1024)}, u32[]{:S(2)}) copy-start(s32[1536]{0:T(1024)} %param.17) | copy-start | bytes 18436
  47.1 7.7 %copy-start.4 = (bf16[384,128]{1,0:T(8,128)(2,1)S(1)}, bf16[384,128]{1,0:T(8,128)(2,1)}, u32[]{:S(2)}) copy-start(bf16[384,128]{1,0:T(8,128)(2,1)} %param.16) | copy-start | bytes 294916
  47.1 16.9 %copy-start.11 = (f32[32]{0:T(128)S(1)}, f32[32]{0:T(128)}, u32[]{:S(2)}) copy-start(f32[32]{0:T(128)} %param.15) | copy-start | bytes 388
  47.2 95.7 %collective-permute-start.4 = (bf16[192,384]{1,0:T(8,128)(2,1)S(1)}, bf16[192,384]{1,0:T(8,128)(2,1)S(1)}, u32[]{:S(2)}, u32[]{:S(2)}) collective-permute-start(bf16[192,384]{1,0:T(8,128)(2,1)S(1)} %get-tuple-element.53), channel_id=1, source_target_pairs={{0,8},{8,16},{16,24},{24,0},{1,9},{9,17},{17,25},{25,1},{2,10},{10... | collective-permute-start | bytes 442376 | tf_op jit(solution)/shard_map/ppermute | solution.py:612
  47.5 95.4 %collective-permute-start.5 = (bf16[192,384]{1,0:T(8,128)(2,1)S(1)}, bf16[192,384]{1,0:T(8,128)(2,1)S(1)}, u32[]{:S(2)}, u32[]{:S(2)}) collective-permute-start(bf16[192,384]{1,0:T(8,128)(2,1)S(1)} %get-tuple-element.54), channel_id=1, source_target_pairs={{0,16},{8,24},{16,0},{24,8},{1,17},{9,25},{17,1},{25,9},{2,18},{10... | collective-permute-start | bytes 442376 | tf_op jit(solution)/shard_map/ppermute | solution.py:612
  49.8 93.1 %collective-permute-start.6 = (bf16[192,384]{1,0:T(8,128)(2,1)S(1)}, bf16[192,384]{1,0:T(8,128)(2,1)S(1)}, u32[]{:S(2)}, u32[]{:S(2)}) collective-permute-start(bf16[192,384]{1,0:T(8,128)(2,1)S(1)} %get-tuple-element.52), channel_id=1, source_target_pairs={{0,24},{8,0},{16,8},{24,16},{1,25},{9,1},{17,9},{25,17},{2,26},{10... | collective-permute-start | bytes 442376 | tf_op jit(solution)/shard_map/ppermute | solution.py:612
  55.0 9.8 %collective-permute-start.3 = (bf16[400,8]{0,1:T(8,128)(2,1)S(1)}, bf16[400,8]{0,1:T(8,128)(2,1)S(1)}, u32[]{:S(2)}, u32[]{:S(2)}) collective-permute-start(bf16[400,8]{0,1:T(8,128)(2,1)S(1)} %get-tuple-element.49), channel_id=1, source_target_pairs={{1,0},{8,1},{9,8},{16,9},{17,16},{24,17},{25,24},{3,2},{10,3},{11,... | collective-permute-start | bytes 19208 | tf_op jit(solution)/shard_map/ppermute | solution.py:23
  56.3 8.5 %collective-permute-start.2 = (bf16[400,8]{0,1:T(8,128)(2,1)S(1)}, bf16[400,8]{0,1:T(8,128)(2,1)S(1)}, u32[]{:S(2)}, u32[]{:S(2)}) collective-permute-start(bf16[400,8]{0,1:T(8,128)(2,1)S(1)} %get-tuple-element.48), channel_id=1, source_target_pairs={{0,1},{1,8},{8,9},{9,16},{16,17},{17,24},{24,25},{2,3},{3,10},{10,... | collective-permute-start | bytes 19208 | tf_op jit(solution)/shard_map/ppermute | solution.py:21
  110.5 1.1 copy-start.7
  111.6 1.2 copy-start.5
  111.6 1.2 copy-start.10
  113.7 25.2 %copy-start.3 = (f32[176,512]{1,0:T(8,128)S(1)}, f32[176,512]{1,0:T(8,128)}, u32[]{:S(2)}) copy-start(f32[176,512]{1,0:T(8,128)} %get-tuple-element.14) | copy-start | bytes 1081348
